TPU v7x, 256 devices: a whole 4x4x8 slice. The times are simulated.
256 devices in a mesh: seq: 16 (over x, y_lo, core), wt: 16 (over y_hi, z).
Axes of the slice: x: 4, y: 4 (y_hi: 2, y_lo: 2; y = y_hi * 2 + y_lo), z: 8, core: 2. Of those that a mesh axis runs over, the one named last changes fastest.
Arguments:
- hidden_states: bfloat16 [4096, 8192], P('seq'), may hold values from -32 to 32
- norm_gain: bfloat16 [8192], replicated, may hold values from 0.099609375 to 1.8984375
- query_weight: bfloat16 [8192, 8192], P('seq', 'wt')
- key_value_matrix: bfloat16 [8192, 2048], P('seq')
- output_weight: bfloat16 [8192, 8192], P('wt', 'seq'), may hold values from -0.0625 to 0.0625
Outputs:
- sublayer_out: bfloat16 [4096, 8192], P('seq', 'wt')
All inputs are finite; a program needn't handle non-finite values.
Results may differ from a plain program's by a relative error of at most 0.0095.
Values may be sent and summed in bfloat16 or wider, within the bound.
A program may use at most 128 MiB of HBM per device.

v0:
```python
import math

import jax
import jax.numpy as jnp
from jax import lax
from jax.sharding import PartitionSpec as P

QUERY_HEADS = 64
KEY_VALUE_HEADS = 8
HEAD_SIZE = 128


def rope_tables(count, offset):
    positions = jnp.arange(count, dtype=jnp.float32) + offset
    exponent = jnp.arange(HEAD_SIZE // 2, dtype=jnp.float32) * (2.0 / HEAD_SIZE)
    inverse = jnp.power(jnp.float32(500000.0), -exponent)
    angles = positions[:, None] * inverse[None, :]
    return (jnp.cos(angles), jnp.sin(angles))


def rotate_half(vectors, cosines, sines):
    half = vectors.shape[-1] // 2
    first = vectors[..., :half]
    second = vectors[..., half:]
    cos_wide = cosines[:, None, :]
    sin_wide = sines[:, None, :]
    return jnp.concatenate(
        [first * cos_wide - second * sin_wide, second * cos_wide + first * sin_wide], axis=-1
    )


def local(hidden_states, norm_gain, query_weight, key_value_matrix, output_weight):
    row_count = hidden_states.shape[0]
    seq_start = lax.axis_index("seq") * row_count
    wt_index = lax.axis_index("wt")
    wt_count = lax.axis_size("wt")
    states = hidden_states.astype(jnp.float32)
    inverse_rms = lax.rsqrt(jnp.mean(states * states, axis=1, keepdims=True) + 1e-05)
    normalized_input = (states * inverse_rms * norm_gain.astype(jnp.float32)[None, :]).astype(
        jnp.bfloat16
    )
    cosines, sines = rope_tables(row_count, seq_start.astype(jnp.float32))
    heads_here = query_weight.shape[1] // HEAD_SIZE
    queries_per_group = QUERY_HEADS // KEY_VALUE_HEADS
    kv_here = max(1, heads_here // queries_per_group)
    per_kv = heads_here // kv_here
    kv_first = wt_index * heads_here // queries_per_group

    def contract(piece):
        return jnp.dot(normalized_input, piece, preferred_element_type=jnp.float32)

    query_raw = contract(lax.all_gather(query_weight, "seq", axis=0, tiled=True))
    queries = rotate_half(
        query_raw.reshape(row_count, heads_here, HEAD_SIZE), cosines, sines
    ).astype(jnp.bfloat16)
    mine = lax.dynamic_slice_in_dim(
        key_value_matrix, kv_first * 2 * HEAD_SIZE, kv_here * 2 * HEAD_SIZE, 1
    )
    projected_rows = contract(lax.all_gather(mine, "seq", axis=0, tiled=True))
    projected_rows = projected_rows.reshape(row_count, kv_here, 2, HEAD_SIZE)
    keys = rotate_half(projected_rows[:, :, 0], cosines, sines).astype(jnp.bfloat16)
    values = projected_rows[:, :, 1].astype(jnp.bfloat16)
    grouped_queries = queries.reshape(row_count, kv_here, per_kv, HEAD_SIZE)
    key_flat = keys.reshape(row_count, kv_here * HEAD_SIZE)
    value_flat = values.reshape(row_count, kv_here * HEAD_SIZE)
    row_ids = seq_start + jnp.arange(row_count, dtype=jnp.int32)
    score_scale = 1.0 / math.sqrt(HEAD_SIZE)
    pieces = (
        lax.all_gather(key_flat, "seq", axis=0, tiled=True),
        lax.all_gather(value_flat, "seq", axis=0, tiled=True),
    )
    highest = jnp.full((kv_here, per_kv, row_count), -1e30, jnp.float32)
    piece_rows = pieces[0].shape[0]
    key_piece = pieces[0].reshape(piece_rows, kv_here, HEAD_SIZE)
    value_piece = pieces[1].reshape(piece_rows, kv_here, HEAD_SIZE)
    scores = (
        jnp.einsum("sagd,nad->agsn", grouped_queries, key_piece, preferred_element_type=jnp.float32)
        * score_scale
    )
    col_ids = jnp.arange(piece_rows, dtype=jnp.int32)
    allowed = (col_ids[None, :] <= row_ids[:, None])[None, None]
    scores = jnp.where(allowed, scores, -1e30)
    new_high = jnp.maximum(highest, jnp.max(scores, axis=-1))
    weights = jnp.where(allowed, jnp.exp(scores - new_high[..., None]), 0.0)
    totals = jnp.sum(weights, axis=-1)
    update = jnp.einsum(
        "agsn,nad->agsd", weights, value_piece.astype(jnp.float32), precision=lax.Precision.HIGHEST
    )
    mixed = update
    highest, totals, mixed = (new_high, totals, mixed)
    attention = (
        jnp.transpose(mixed / totals[..., None], (2, 0, 1, 3))
        .reshape(row_count, heads_here * HEAD_SIZE)
        .astype(jnp.bfloat16)
    )
    out_width = hidden_states.shape[1] // wt_count
    residual_cols = lax.dynamic_slice_in_dim(states, wt_index * out_width, out_width, 1)
    terms = jnp.dot(
        attention,
        lax.all_gather(output_weight, "seq", axis=1, tiled=True),
        preferred_element_type=jnp.float32,
    )
    summed = lax.psum_scatter(
        terms.astype(jnp.bfloat16), "wt", scatter_dimension=1, tiled=True
    ).astype(jnp.float32)
    return (residual_cols + summed).astype(jnp.bfloat16)


def solution(mesh):
    in_specs = (P("seq", None), P(), P("seq", "wt"), P("seq", None), P("wt", "seq"))
    out_specs = P("seq", "wt")
    return jax.shard_map(local, mesh=mesh, in_specs=in_specs, out_specs=out_specs, check_vma=False)
```

profile of v0, /device:TPU:1, one launch (start us, length us, event | category | flops | bytes accessed | tf_op | source)
XLA Modules:
  0.0 467.7 jit_solution(580025353465871369)
XLA Ops:
  6.5 1.6 copy-done
  8.1 0.7 constant_dynamic-slice_fusion
  8.9 0.0 all-gather.11.cloned.1.call-start
  8.9 0.7 all-gather.11.cloned.1.call-update
  9.7 0.7 convert_element_type.49
  10.4 3.1 multiply_reduce_fusion
  13.6 39.8 %all-gather.7.cloned.1.call-done = bf16[8192,256]{1,0:T(8,128)(2,1)} async-done(((bf16[512,256]{1,0:T(8,128)(2,1)}), bf16[8192,256]{1,0:T(8,128)(2,1)}) %all-gather.7.cloned.1.call-update) | async-done | bytes 4194320 | tf_op jit(solution)/shard_map/all_gather | solution.py:59
  53.3 5.5 %fusion.10 = f32[256,256]{0,1:T(8,128)S(1)} fusion(bf16[8192,256]{1,0:T(8,128)(2,1)} %all-gather.7.cloned.1.call-done, f32[8192]{0:T(1024)S(1)} %convert_element_type.49, f32[256]{0:T(256)S(1)} %add_rsqrt_fusion, bf16[256,8192]{1,0:T(8,128)(2,1)} %param.5), kind=kOutput, calls=%fused_computation.16 | convolution fusion | flops 1082130432 | bytes 8684544 | tf_op jit(solution)/shard_map/dot_general | solution.py:50
  58.9 0.1 copy.11
  59.0 0.6 fusion.36
  59.6 0.7 pad_maximum_fusion
  60.3 0.0 all-gather.15.cloned.1.call-start
  60.4 0.6 slice.44
  61.1 0.5 all-gather.13.cloned.1.call-update
  61.7 0.5 multiply_cosine_fusion
  62.2 1.7 iota_compare_fusion
  63.9 46.1 %all-gather.11.cloned.1.call-done = bf16[8192,512]{1,0:T(8,128)(2,1)} async-done(((bf16[512,512]{1,0:T(8,128)(2,1)}), bf16[8192,512]{1,0:T(8,128)(2,1)}) %all-gather.11.cloned.1.call-update) | async-done | bytes 8388624 | tf_op jit(solution)/shard_map/all_gather | solution.py:52
  110.0 7.0 %fusion.9 = f32[256,512]{1,0:T(8,128)S(1)} fusion(bf16[8192,512]{1,0:T(8,128)(2,1)} %all-gather.11.cloned.1.call-done, f32[8192]{0:T(1024)S(1)} %convert_element_type.49, f32[256]{0:T(256)S(1)} %add_rsqrt_fusion, bf16[256,8192]{1,0:T(8,128)(2,1)} %param.5), kind=kOutput, calls=%fused_computation.15 | convolution fusion | flops 2155872256 | bytes 13140992 | tf_op jit(solution)/shard_map/dot_general | solution.py:50
  117.0 0.2 reshape.203
  117.2 0.3 fusion.41
  117.5 0.8 subtract_convert_fusion
  118.4 29.3 %all-gather.9.cloned.1.call-done = bf16[4096,128]{1,0:T(8,128)(2,1)} async-done(((bf16[256,128]{1,0:T(8,128)(2,1)}), bf16[4096,128]{1,0:T(8,128)(2,1)}) %all-gather.9.cloned.1.call-update) | async-done | bytes 1048592 | tf_op jit(solution)/shard_map/all_gather | solution.py:69
  147.7 4.5 fusion.2
  152.2 5.7 %copy-done.1 = f32[4096,256,4]{1,0,2:T(8,128)} copy-done((f32[4096,256,4]{1,0,2:T(8,128)}, f32[4096,256,4]{1,0,2:T(8,128)S(1)}, u32[]{:S(2)}) %copy-start.1) | copy-done | bytes 16777240
  158.0 4.2 fusion.3
  162.2 23.8 %all-gather.15.cloned.1.call-done = bf16[4096,1,1,128]{0,3,2,1:T(8,128)(2,1)} async-done(((bf16[256,1,1,128]{0,3,2,1:T(8,128)(2,1)}), bf16[4096,1,1,128]{0,3,2,1:T(8,128)(2,1)}) %all-gather.15.cloned.1.call-update) | async-done | bytes 1048592 | tf_op jit(solution)/shard_map/all_gather | solution.py:70
  186.0 13.0 %fusion.19 = bf16[4,256,128]{1,2,0:T(8,128)(2,1)S(1)} fusion(bf16[4096,1,1,128]{0,3,2,1:T(8,128)(2,1)} %all-gather.15.cloned.1.call-done, f32[4096,256,4]{1,0,2:T(8,128)} %copy-done.1, f32[4,256]{1,0:T(4,128)S(1)} %broadcast_maximum_fusion, pred[256,4096]{0,1:T(8,128)(4,1)S(1)} %copy-done.2, f32[4,256]{1,0:T(4,128)S(1)} %fusion.3), kind=kOutput, calls=%fused_computation.21 | convolution fusion | flops 6459490304 | bytes 19144704 | tf_op jit(solution)/shard_map/agsn,nad->agsd/dot_general | solution.py:86
  199.0 43.5 %all-gather.13.cloned.1.call-done = bf16[512,8192]{1,0:T(8,128)(2,1)} async-done(((bf16[512,512]{1,0:T(8,128)(2,1)}), bf16[512,8192]{1,0:T(8,128)(2,1)}) %all-gather.13.cloned.1.call-update) | async-done | bytes 8388624 | tf_op jit(solution)/shard_map/all_gather | solution.py:100
  242.5 7.7 %convolution_convert_fusion = bf16[256,8192]{1,0:T(8,128)(2,1)} fusion(bf16[256,512]{0,1:T(8,128)(2,1)S(1)} %bitcast.54, bf16[512,8192]{1,0:T(8,128)(2,1)} %all-gather.13.cloned.1.call-done), kind=kOutput, calls=%fused_computation.6 | convolution fusion | flops 2149580800 | bytes 12845056 | tf_op jit(solution)/shard_map/dot_general | solution.py:98
  250.3 6.4 %convert_element_type.48 = f32[256,8192]{1,0:T(8,128)} convert(bf16[256,8192]{1,0:T(8,128)(2,1)} %param.5) | non-fusion elementwise | flops 2097152 | bytes 12582912 | tf_op jit(solution)/shard_map/convert_element_type | solution.py:37
  256.7 202.3 %reduce-scatter.2.cloned.1.call-done = bf16[256,512]{1,0:T(8,128)(2,1)} async-done(((bf16[256,8192]{1,0:T(8,128)(2,1)}), bf16[256,512]{1,0:T(8,128)(2,1)}) %reduce-scatter.2.cloned.1.call-update) | async-done | bytes 262160 | tf_op jit(solution)/shard_map/reduce_scatter | solution.py:103
  459.0 1.9 add_convert_fusion
  (18 shorter events, 0.2 us)
Async XLA Ops:
  6.5 1.6 copy-start
  6.5 46.8 %all-gather.7.cloned.1.call-start = ((), (), s32[]{:S(2)}) async-start(), calls=%async_computation.1 | async-start | bytes 4456448 | tf_op jit(solution)/shard_map/all_gather | solution.py:59
  8.9 101.1 %all-gather.11.cloned.1.call-start = ((), (), s32[]{:S(2)}) async-start(), calls=%async_computation.3 | async-start | bytes 8912896 | tf_op jit(solution)/shard_map/all_gather | solution.py:52
  9.6 138.1 %all-gather.9.cloned.1.call-start = ((), (), s32[]{:S(2)}) async-start(), calls=%async_computation.2 | async-start | bytes 1114112 | tf_op jit(solution)/shard_map/all_gather | solution.py:69
  60.3 125.7 %all-gather.15.cloned.1.call-start = ((), (), s32[]{:S(2)}) async-start(), calls=%async_computation.6 | async-start | bytes 1114112 | tf_op jit(solution)/shard_map/all_gather | solution.py:70
  61.0 181.5 %all-gather.13.cloned.1.call-start = ((), (), s32[]{:S(2)}) async-start(), calls=%async_computation.4 | async-start | bytes 8912896 | tf_op jit(solution)/shard_map/all_gather | solution.py:100
  61.6 397.3 %reduce-scatter.2.cloned.1.call-start = ((), (), s32[]{:S(2)}) async-start(), calls=%async_computation.5 | async-start | bytes 4456448 | tf_op jit(solution)/shard_map/reduce_scatter | solution.py:103
  147.7 10.3 %copy-start.2 = (pred[256,4096]{0,1:T(8,128)(4,1)S(1)}, pred[256,4096]{0,1:T(8,128)(4,1)}, u32[]{:S(2)}) copy-start(pred[256,4096]{0,1:T(8,128)(4,1)} %iota_compare_fusion) | copy-start | bytes 3145732
  152.2 5.7 %copy-start.1 = (f32[4096,256,4]{1,0,2:T(8,128)}, f32[4096,256,4]{1,0,2:T(8,128)S(1)}, u32[]{:S(2)}) copy-start(f32[4096,256,4]{1,0,2:T(8,128)S(1)} %get-tuple-element.14) | copy-start | bytes 50331652
Sparse Core Ops, SparseCore 0:
  9.2 44.0 all-gather.6
  55.2 54.7 all-gather.10
  111.8 35.8 all-gather.8
  149.3 36.6 all-gather.14
  187.6 54.8 all-gather.12
  250.4 208.5 reduce-scatter.1
where the time goes:
time: 472 us; the launch traced here: 468 us
  waiting for transfers between devices  386 us (82%)
  matrix products  37.8 us (8%)
  other arithmetic  20.7 us (4%)
  between operations  13.6 us (3%)
  local copies, waits for them, and re-layouts  9.31 us (2%)
    reduce_scatter x1, waiting for transfers between devices, local(): lax.psum_scatter(terms.astype(jnp.bfloat16), 'wt', scatter_dimension=1, t...  202 us
    all_gather x1, waiting for transfers between devices, local(): lax.all_gather(query_weight, 'seq', axis=0, tiled=True)  46.1 us
    all_gather x1, waiting for transfers between devices, local(): lax.all_gather(output_weight, 'seq', axis=1, tiled=True)  43.5 us
    all_gather x1, waiting for transfers between devices, local(): projected_rows = contract(lax.all_gather(mine, 'seq', axis=0, tiled=True))  39.8 us
    all_gather x1, waiting for transfers between devices, local(): lax.all_gather(key_flat, 'seq', axis=0, tiled=True)  29.3 us
    all_gather x1, waiting for transfers between devices, local(): lax.all_gather(value_flat, 'seq', axis=0, tiled=True)  23.8 us
    dot_general x1, matrix products, local(): jnp.einsum('agsn,nad->agsd', weights, value_piece.astype(jnp.float32), pr...  13 us
    dot_general x2, matrix products, contract(): return jnp.dot(normalized_input, piece, preferred_element_type=jnp.float32)  12.6 us
  transfers between devices with their start and end apart: 6, of which 6 were waited for; matrix products, arithmetic and copies ran while one was open for 11% of the time, Pallas kernels for 0%

commit v1 on v0

v1 whole, which is shorter than its diff:
```python
import math

import jax
import jax.numpy as jnp
import numpy as np
from jax import lax
from jax.experimental import pallas as pl
from jax.experimental.pallas import tpu as pltpu
from jax.sharding import PartitionSpec as P

MESH = pl.DeviceIdType.MESH
HEAD = 128
ROWS = 256
SHARDS = 16
BLOCK = 512
HEADS_HERE = 4
SCORE_LOG2 = math.log2(math.e) / math.sqrt(HEAD)
KV_WEIGHT, QUERY, OUTPUT, KEYS = 0, 1, 2, 3
f32 = jnp.float32
bf16 = jnp.bfloat16


def rope_constants():
    inverse = 500000.0 ** (-np.arange(HEAD // 2) * 2.0 / HEAD)
    wide = np.concatenate([inverse, inverse])
    sign = np.concatenate([-np.ones(HEAD // 2), np.ones(HEAD // 2)])
    inner = np.arange(ROWS)[:, None] * wide[None, :]
    outer = (np.arange(SHARDS) * ROWS)[:, None] * wide[None, :]
    tables = (np.cos(inner), np.sin(inner) * sign, np.cos(outer), np.sin(outer) * sign)
    return [t.astype(np.float32) for t in tables]


def body(
    hidden_ref, gain_ref, wq_ref, wkv_ref, wo_ref, cr_ref, sr_ref, cb_ref, sb_ref,
    out_ref,
    hid, normed, wkv, wq, wo, kv, qacc, qrot, macc, oacc, attn,
    snd4, rcv4, snd, rcv, ysnd, yrcv, total,
    gsend, grecv, rsend, rrecv, xsend, xrecv, lsem,
):
    s = lax.axis_index("seq")
    w = lax.axis_index("wt")
    x, yl, core = lax.div(s, 4), lax.rem(lax.div(s, 2), 2), lax.rem(s, 2)
    yh, z = lax.div(w, 8), lax.rem(w, 8)
    xp, xm, xo = lax.rem(x + 1, 4), lax.rem(x + 3, 4), lax.rem(x + 2, 4)
    yp, sib_core = 1 - yl, 1 - core
    par = lax.rem(z, 2)
    chip = lax.div(s, 2)

    def sid(xi, yi, ci):
        return (xi * 2 + yi) * 2 + ci

    def wid(yi, zi):
        return yi * 8 + zi

    to_xp, to_xm = (sid(xp, yl, core), w), (sid(xm, yl, core), w)
    to_y, to_sib = (sid(x, yp, core), w), (sid(x, yl, sib_core), w)
    to_zp, to_zm = (s, wid(yh, lax.rem(z + 1, 8))), (s, wid(yh, lax.rem(z + 7, 8)))
    to_yh = (s, wid(1 - yh, z))
    to_pair = (s, wid(yh, z + 1 - 2 * par))

    barrier = pltpu.get_barrier_semaphore()
    for peer in (to_xp, to_xm, to_y, to_sib, to_zp, to_zm, to_yh):
        pl.semaphore_signal(barrier, inc=1, device_id=peer, device_id_type=MESH)

    first = pltpu.make_async_copy(
        wkv_ref.at[:, pl.ds(pl.multiple_of(w * HEAD, HEAD), HEAD)], wkv.at[s], lsem.at[0]
    )
    load_hidden = pltpu.make_async_copy(hidden_ref, hid, lsem.at[1])
    load_q = pltpu.make_async_copy(wq_ref, wq.at[s], lsem.at[2])
    load_o = pltpu.make_async_copy(wo_ref, wo.at[s], lsem.at[3])
    first.start()
    load_hidden.start()
    load_q.start()
    load_o.start()
    pl.semaphore_wait(barrier, 7)

    stores = {KV_WEIGHT: wkv, QUERY: wq, OUTPUT: wo}

    def slot(k, shard, half=None):
        if k == KEYS:
            rows = pl.ds(pl.multiple_of(shard * ROWS, ROWS), ROWS)
            return kv.at[:, rows] if half is None else kv.at[half, rows]
        if half is None:
            return stores[k].at[shard]
        return stores[k].at[shard, pl.ds(half * 256, 256)]

    started = []

    def send(k, label, source, place, peer):
        copy = pltpu.make_async_remote_copy(
            src_ref=source, dst_ref=place, send_sem=gsend.at[k, label], recv_sem=grecv.at[k, label],
            device_id=peer, device_id_type=MESH,
        )
        copy.start()
        started.append(copy)

    def forward(k, label, shard, peer, half=None):
        send(k, label, slot(k, shard, half), slot(k, shard, half), peer)

    def arrive(k, label, shard, half=None):
        place = slot(k, shard, half)
        pltpu.make_async_remote_copy(
            src_ref=place, dst_ref=place, send_sem=gsend.at[k, label], recv_sem=grecv.at[k, label],
            device_id=to_sib, device_id_type=MESH,
        ).wait_recv()

    chips = [(x, yl), (x, yp), (xm, yl), (xp, yl), (xm, yp), (xp, yp), (xo, yl), (xo, yp)]
    mine = [sid(a, b, core) for a, b in chips]
    theirs = [sid(a, b, sib_core) for a, b in chips]
    sib_label = [3, 9, 10, 11, 12, 13, 14, 15]

    def own_sends(k, source):
        for label, peer in ((0, to_xp), (1, to_xm), (2, to_y), (3, to_sib)):
            send(k, label, source, slot(k, s), peer)

    def near(k):
        arrive(k, 0, mine[2])
        forward(k, 6, mine[2], to_xp, 0)
        arrive(k, 1, mine[3])
        forward(k, 7, mine[3], to_xm, 1)
        arrive(k, 2, mine[1])
        forward(k, 4, mine[1], to_xp)
        forward(k, 5, mine[1], to_xm)
        for p in (1, 2, 3):
            forward(k, sib_label[p], mine[p], to_sib)

    def middle(k):
        arrive(k, 6, mine[6], 0)
        arrive(k, 7, mine[6], 1)
        forward(k, 8, mine[6], to_y)
        forward(k, sib_label[6], mine[6], to_sib)
        arrive(k, 4, mine[4])
        forward(k, sib_label[4], mine[4], to_sib)
        arrive(k, 5, mine[5])
        forward(k, sib_label[5], mine[5], to_sib)

    def far(k):
        arrive(k, 8, mine[7])
        forward(k, sib_label[7], mine[7], to_sib)

    def from_sib(k, p):
        arrive(k, sib_label[p], theirs[p])

    first.wait()
    own_sends(KV_WEIGHT, wkv.at[s])
    own_sends(QUERY, wq_ref)

    load_hidden.wait()

    def square(i, acc):
        block = hid[:, pl.ds(pl.multiple_of(i * BLOCK, BLOCK), BLOCK)].astype(f32)
        block = block * block
        return acc + (block[:, :128] + block[:, 128:256]) + (block[:, 256:384] + block[:, 384:])

    squares = lax.fori_loop(0, SHARDS, square, jnp.zeros((ROWS, 128), f32))
    inverse = lax.rsqrt(jnp.sum(squares, axis=1, keepdims=True) * (1.0 / 8192.0) + 1e-05)

    near(KV_WEIGHT)

    def scale(i, _):
        columns = pl.ds(pl.multiple_of(i * BLOCK, BLOCK), BLOCK)
        block = hid[:, columns].astype(f32) * inverse * gain_ref[:, columns].astype(f32)
        normed[i] = block.astype(bf16)
        return 0

    lax.fori_loop(0, SHARDS, scale, 0)
    middle(KV_WEIGHT)
    far(KV_WEIGHT)

    for p in range(8):
        from_sib(KV_WEIGHT, p)

    def project(i, acc):
        return acc + jnp.dot(normed[i], wkv[i], preferred_element_type=f32)

    raw = lax.fori_loop(0, SHARDS, project, jnp.zeros((ROWS, HEAD), f32))
    near(QUERY)
    base = pl.ds(s, 1)
    cosines = cb_ref[base, :] * cr_ref[...] - sb_ref[base, :] * sr_ref[...]
    sines = sb_ref[base, :] * cr_ref[...] + cb_ref[base, :] * sr_ref[...]

    def rotate(u):
        return u * cosines + pltpu.roll(u, HEAD // 2, 1) * sines

    rows_here = pl.ds(pl.multiple_of(s * ROWS, ROWS), ROWS)
    is_value = (lax.broadcasted_iota(jnp.int32, (ROWS, HEAD), 0) * 0 + par) == 1
    kv[par, rows_here] = jnp.where(is_value, raw, rotate(raw)).astype(bf16)
    pair = pltpu.make_async_remote_copy(
        src_ref=kv.at[par, rows_here], dst_ref=kv.at[par, rows_here], send_sem=xsend.at[0], recv_sem=xrecv.at[0],
        device_id=to_pair, device_id_type=MESH,
    )
    pair.start()
    started.append(pair)
    load_q.wait()

    def accumulate(shard, start=False):
        term = jnp.dot(normed[shard], wq[shard], preferred_element_type=f32)
        qacc[...] = term if start else qacc[...] + term

    accumulate(mine[0], True)
    pltpu.make_async_remote_copy(
        src_ref=kv.at[1 - par, rows_here], dst_ref=kv.at[1 - par, rows_here], send_sem=xsend.at[0],
        recv_sem=xrecv.at[0], device_id=to_pair, device_id_type=MESH,
    ).wait_recv()
    own_sends(KEYS, slot(KEYS, s))
    for p in (1, 2, 3):
        accumulate(mine[p])
    near(KEYS)
    own_sends(OUTPUT, wo_ref)
    for p in (0, 1, 2, 3):
        from_sib(QUERY, p)
        accumulate(theirs[p])
    middle(QUERY)
    middle(KEYS)
    for p in (4, 5, 6):
        accumulate(mine[p])
    far(KEYS)
    far(QUERY)
    for p in (4, 5, 6):
        from_sib(QUERY, p)
        accumulate(theirs[p])
    accumulate(mine[7])
    from_sib(QUERY, 7)
    accumulate(theirs[7])
    for h in range(HEADS_HERE):
        qrot[h] = rotate(qacc[:, h * HEAD : (h + 1) * HEAD]).astype(bf16)
    for p in range(8):
        from_sib(KEYS, p)

    ones = jnp.ones((BLOCK, HEAD), bf16)

    def scores_of(h, block):
        rows = pl.ds(pl.multiple_of(block * BLOCK, BLOCK), BLOCK)
        return lax.dot_general(
            qrot[h], kv[0, rows], (((1,), (1,)), ((), ())), preferred_element_type=f32
        )

    def values_of(block):
        rows = pl.ds(pl.multiple_of(block * BLOCK, BLOCK), BLOCK)
        return jnp.concatenate([kv[1, rows], ones], axis=1)

    query_at = lax.broadcasted_iota(jnp.int32, (ROWS, BLOCK), 0) + core * ROWS
    allowed = lax.broadcasted_iota(jnp.int32, (ROWS, BLOCK), 1) <= query_at
    for h in range(HEADS_HERE):
        scores = jnp.where(allowed, scores_of(h, chip), -1e30)
        high = jnp.max(scores, axis=1, keepdims=True)
        weights = jnp.exp2((scores - high) * SCORE_LOG2).astype(bf16)
        oacc[h] = jnp.dot(weights, values_of(chip), preferred_element_type=f32)
        macc[h] = jnp.broadcast_to(high, (ROWS, HEAD))

    def attend(block, _):
        values = values_of(block)
        for h in range(HEADS_HERE):
            scores = scores_of(h, block)
            before = macc[h][:, :1]
            high = jnp.maximum(before, jnp.max(scores, axis=1, keepdims=True))
            weights = jnp.exp2((scores - high) * SCORE_LOG2).astype(bf16)
            keep = jnp.exp2((before - high) * SCORE_LOG2)
            oacc[h] = oacc[h] * keep + jnp.dot(weights, values, preferred_element_type=f32)
            macc[h] = jnp.broadcast_to(high, (ROWS, HEAD))
        return 0

    near(OUTPUT)
    lax.fori_loop(0, jnp.minimum(chip, 4), attend, 0)
    middle(OUTPUT)
    lax.fori_loop(4, jnp.maximum(chip, 4), attend, 0)
    for h in range(HEADS_HERE):
        attn[:, h * HEAD : (h + 1) * HEAD] = (oacc[h][:, :HEAD] / oacc[h][:, HEAD:]).astype(bf16)
    far(OUTPUT)
    load_o.wait()
    for p in range(8):
        from_sib(OUTPUT, p)

    def partial(yi, zi):
        return jnp.dot(attn[...], wo[wid(yi, zi)], preferred_element_type=f32)

    order = (1 - yh, yh)

    def hop(label, source, place, peer):
        copy = pltpu.make_async_remote_copy(
            src_ref=source, dst_ref=place, send_sem=rsend.at[label], recv_sem=rrecv.at[label],
            device_id=peer, device_id_type=MESH,
        )
        copy.start()
        started.append(copy)

    def landed(label, place):
        pltpu.make_async_remote_copy(
            src_ref=place, dst_ref=place, send_sem=rsend.at[label], recv_sem=rrecv.at[label],
            device_id=to_sib, device_id_type=MESH,
        ).wait_recv()

    halves = (pl.ds(0, 128), pl.ds(128, 128))
    ways = (to_zp, to_zm)
    for j in range(2):
        snd4[j] = partial(order[j], lax.rem(z + 4, 8)).astype(bf16)
        for way in range(2):
            hop(way * 2 + j, snd4.at[j, halves[way]], rcv4.at[j, halves[way]], ways[way])
    for d in (3, 2, 1):
        for j in range(2):
            for way in range(2):
                at = lax.rem(z + d, 8) if way == 0 else lax.rem(z + 8 - d, 8)
                term = partial(order[j], at)
                if d == 3:
                    landed(way * 2 + j, rcv4.at[j, halves[way]])
                    got = rcv4[j, halves[way]].astype(f32)
                    if way == 0:
                        snd[d - 1, way, j, :128] = (term[:128] + got).astype(bf16)
                        snd[d - 1, way, j, 128:] = term[128:].astype(bf16)
                    else:
                        snd[d - 1, way, j, :128] = term[:128].astype(bf16)
                        snd[d - 1, way, j, 128:] = (term[128:] + got).astype(bf16)
                else:
                    landed((4 - d - 1) * 4 + way * 2 + j, rcv.at[d, way, j])
                    snd[d - 1, way, j] = (term + rcv[d, way, j].astype(f32)).astype(bf16)
                hop((4 - d) * 4 + way * 2 + j, snd.at[d - 1, way, j], rcv.at[d - 1, way, j], ways[way])
    for j in range(2):
        term = partial(order[j], z)
        for way in range(2):
            landed(12 + way * 2 + j, rcv.at[0, way, j])
            term = term + rcv[0, way, j].astype(f32)
        if j == 0:
            ysnd[...] = term.astype(bf16)
            hop(16, ysnd, yrcv, to_yh)
        else:
            columns = pl.ds(pl.multiple_of(w * BLOCK, BLOCK), BLOCK)
            total[...] = term + hid[:, columns].astype(f32)
    landed(16, yrcv)
    out_ref[...] = (total[...] + yrcv[...].astype(f32)).astype(bf16)
    for copy in started:
        copy.wait_send()


def local(hidden_states, norm_gain, query_weight, key_value_matrix, output_weight):
    tables = [jnp.asarray(t) for t in rope_constants()]
    anywhere = pl.BlockSpec(memory_space=pl.ANY)
    inside = pl.BlockSpec(memory_space=pltpu.VMEM)
    dma = pltpu.SemaphoreType.DMA
    return pl.pallas_call(
        body,
        out_shape=jax.ShapeDtypeStruct((ROWS, BLOCK), bf16),
        in_specs=[anywhere, inside, anywhere, anywhere, anywhere] + [inside] * 4,
        out_specs=inside,
        scratch_shapes=[
            pltpu.VMEM((ROWS, 8192), bf16),
            pltpu.VMEM((SHARDS, ROWS, BLOCK), bf16),
            pltpu.VMEM((SHARDS, BLOCK, HEAD), bf16),
            pltpu.VMEM((SHARDS, BLOCK, BLOCK), bf16),
            pltpu.VMEM((SHARDS, BLOCK, BLOCK), bf16),
            pltpu.VMEM((2, SHARDS * ROWS, HEAD), bf16),
            pltpu.VMEM((ROWS, BLOCK), f32),
            pltpu.VMEM((HEADS_HERE, ROWS, HEAD), bf16),
            pltpu.VMEM((HEADS_HERE, ROWS, HEAD), f32),
            pltpu.VMEM((HEADS_HERE, ROWS, 2 * HEAD), f32),
            pltpu.VMEM((ROWS, BLOCK), bf16),
            pltpu.VMEM((2, ROWS, BLOCK), bf16),
            pltpu.VMEM((2, ROWS, BLOCK), bf16),
            pltpu.VMEM((3, 2, 2, ROWS, BLOCK), bf16),
            pltpu.VMEM((3, 2, 2, ROWS, BLOCK), bf16),
            pltpu.VMEM((ROWS, BLOCK), bf16),
            pltpu.VMEM((ROWS, BLOCK), bf16),
            pltpu.VMEM((ROWS, BLOCK), f32),
            dma((4, 16)),
            dma((4, 16)),
            dma((17,)),
            dma((17,)),
            dma((1,)),
            dma((1,)),
            dma((4,)),
        ],
        compiler_params=pltpu.CompilerParams(
            collective_id=0, has_side_effects=True, vmem_limit_bytes=56 * 1024 * 1024
        ),
    )(hidden_states, norm_gain.reshape(1, -1), query_weight, key_value_matrix, output_weight, *tables)


def solution(mesh):
    in_specs = (P("seq", None), P(), P("seq", "wt"), P("seq", None), P("wt", "seq"))
    return jax.shard_map(local, mesh=mesh, in_specs=in_specs, out_specs=P("seq", "wt"), check_vma=False)
```

time: 472 us -> 164 us (0.35)
  waiting for transfers between devices: 386 us -> 0 us
  Pallas kernels: 0 us -> 161 us
  matrix products: 37.8 us -> 0 us
  other arithmetic: 20.7 us -> 0 us
  between operations: 13.6 us -> 0.01 us
  local copies, waits for them, and re-layouts: 9.31 us -> 3.02 us
    reduce_scatter x1 -> x0, waiting for transfers between devices: 202 us -> none  [local(): lax.psum_scatter(terms.astype(jnp.bfloat16), 'wt', scatter_dimension=1, t...]
    all_gather x5 -> x0, waiting for transfers between devices: 182 us -> none  [the longest x1 46.1 us: local(): lax.all_gather(query_weight, 'seq', axis=0, tiled=True)]
    pallas_call x0 -> x1, Pallas kernels: none -> 161 us  [local(): pl.pallas_call(body, out_shape=jax.ShapeDtypeStruct((ROWS, BLOCK), bf16),...]
    dot_general x5 -> x0, matrix products: 37.8 us -> none  [the longest x1 13 us: local(): jnp.einsum('agsn,nad->agsd', weights, value_piece.astype(jnp.float32), pr...]
    convert_element_type x3 -> x0, other arithmetic: 9.02 us -> none  [the longest x1 6.41 us: local(): states = hidden_states.astype(jnp.float32)]
    reduce_sum x2 -> x0, other arithmetic: 7.3 us -> none  [the longest x1 4.19 us: local(): totals = jnp.sum(weights, axis=-1)]
    unnamed x7 -> x1, local copies, waits for them, and re-layouts: 7.4 us -> 1.67 us
  transfers between devices with their start and end apart: 6 -> 0, of which waited for: 6 -> 0; matrix products, arithmetic and copies ran while one was open for 11% -> 0% of each run, Pallas kernels for 0% -> 0%
where the time goes in v1:
time: 164 us
  Pallas kernels  161 us (98%)
  local copies, waits for them, and re-layouts  3.02 us (2%)
    pallas_call x1, Pallas kernels, local(): pl.pallas_call(body, out_shape=jax.ShapeDtypeStruct((ROWS, BLOCK), bf16),...  161 us

profile of v1, /device:TPU:1, one launch (start us, length us, event | category | flops | bytes accessed | tf_op | source)
XLA Modules:
  0.0 163.7 jit_solution(12468548541273440821)
XLA Ops:
  0.0 1.3 reshape.3.gain_ref
  1.4 160.7 %shard_map.91 = bf16[256,512]{1,0:T(8,128)(2,1)} custom-call(bf16[256,8192]{1,0:T(8,128)(2,1)} %hidden_ref.1, bf16[1,8192]{1,0:T(2,128)(2,1)} %reshape.3.gain_ref, bf16[512,512]{1,0:T(8,128)(2,1)} %wq_ref.1, bf16[512,2048]{1,0:T(8,128)(2,1)} %wkv_ref.1, bf16[512,512]{1,0:T(8,128)(2,1)} %wo_ref.1, f32[256,128]{1,0:T(8,128)} %constant.8.clone.cr_ref, ...), custom_call_target="tpu_custom_call" | custom-call | tf_op jit(solution)/shard_map/pallas_call | solution.py:339
  162.0 1.7 %copy.11 = bf16[256,512]{1,0:T(8,128)(2,1)} copy(bf16[256,512]{1,0:T(8,128)(2,1)} %shard_map.91) | data formatting | bytes 524288

commit v2 on v1

--- a/solution.py
+++ b/solution.py
@@ -33,9 +33,8 @@
 def body(
     hidden_ref, gain_ref, wq_ref, wkv_ref, wo_ref, cr_ref, sr_ref, cb_ref, sb_ref,
     out_ref,
-    hid, normed, wkv, wq, wo, kv, qacc, qrot, macc, oacc, attn,
-    snd4, rcv4, snd, rcv, ysnd, yrcv, total,
-    gsend, grecv, rsend, rrecv, xsend, xrecv, lsem,
+    hid, normed, wkv, wq, wo, kv, qacc, qrot, macc, oacc, heads, tacc, ysnd, yrcv,
+    gsend, grecv, rsend, rrecv, dsend, drecv, xsend, xrecv, lsem,
 ):
     s = lax.axis_index("seq")
     w = lax.axis_index("wt")
@@ -61,18 +60,29 @@
     barrier = pltpu.get_barrier_semaphore()
     for peer in (to_xp, to_xm, to_y, to_sib, to_zp, to_zm, to_yh):
         pl.semaphore_signal(barrier, inc=1, device_id=peer, device_id_type=MESH)
+    keeps_piece = lax.rem(s, 8) == z
+    deal_label = lax.div(s, 8) * 8 + z
+
+    def greet(label):
+        dealer = (z + 8 * lax.div(label, 8), wid(yh, lax.rem(label, 8)))
+        pl.semaphore_signal(barrier, inc=1, device_id=dealer, device_id_type=MESH)
+
+    for i in range(1, SHARDS):
+        greet(lax.rem(deal_label + i, SHARDS))
+
+    @pl.when(jnp.logical_not(keeps_piece))
+    def _():
+        greet(deal_label)
 
     first = pltpu.make_async_copy(
         wkv_ref.at[:, pl.ds(pl.multiple_of(w * HEAD, HEAD), HEAD)], wkv.at[s], lsem.at[0]
     )
     load_hidden = pltpu.make_async_copy(hidden_ref, hid, lsem.at[1])
     load_q = pltpu.make_async_copy(wq_ref, wq.at[s], lsem.at[2])
-    load_o = pltpu.make_async_copy(wo_ref, wo.at[s], lsem.at[3])
     first.start()
     load_hidden.start()
     load_q.start()
-    load_o.start()
-    pl.semaphore_wait(barrier, 7)
+    pl.semaphore_wait(barrier, 7 + SHARDS - jnp.where(keeps_piece, 1, 0))
 
     stores = {KV_WEIGHT: wkv, QUERY: wq, OUTPUT: wo}
 
@@ -82,6 +92,8 @@
             return kv.at[:, rows] if half is None else kv.at[half, rows]
         if half is None:
             return stores[k].at[shard]
+        if k == OUTPUT:
+            return wo.at[shard, half]
         return stores[k].at[shard, pl.ds(half * 256, 256)]
 
     started = []
@@ -145,6 +157,49 @@
     own_sends(KV_WEIGHT, wkv.at[s])
     own_sends(QUERY, wq_ref)
 
+    def piece(p):
+        return wo_ref.at[
+            pl.ds(pl.multiple_of(lax.div(p, 4) * HEAD, HEAD), HEAD), pl.ds(pl.multiple_of(lax.rem(p, 4) * HEAD, HEAD), HEAD)
+        ]
+
+    def deal(i):
+        p = lax.rem(s + i, SHARDS)
+        return pltpu.make_async_remote_copy(
+            src_ref=piece(p), dst_ref=wo.at[p, lax.div(s, 8), z], send_sem=dsend.at[i], recv_sem=drecv.at[deal_label],
+            device_id=(p, wid(yh, lax.rem(s, 8))), device_id_type=MESH,
+        )
+
+    kept = pltpu.make_async_copy(piece(s), wo.at[s, lax.div(s, 8), z], lsem.at[3])
+    for i in range(1, SHARDS):
+        deal(i).start()
+
+    @pl.when(keeps_piece)
+    def _():
+        kept.start()
+
+    @pl.when(jnp.logical_not(keeps_piece))
+    def _():
+        deal(0).start()
+
+    def dealt(label):
+        place = wo.at[s, lax.div(label, 8), lax.rem(label, 8)]
+        pltpu.make_async_remote_copy(
+            src_ref=place, dst_ref=place, send_sem=dsend.at[0], recv_sem=drecv.at[label], device_id=to_sib,
+            device_id_type=MESH,
+        ).wait_recv()
+
+    def all_dealt():
+        for i in range(1, SHARDS):
+            dealt(lax.rem(deal_label + i, SHARDS))
+
+        @pl.when(keeps_piece)
+        def _():
+            kept.wait()
+
+        @pl.when(jnp.logical_not(keeps_piece))
+        def _():
+            dealt(deal_label)
+
     load_hidden.wait()
 
     def square(i, acc):
@@ -206,11 +261,12 @@
     for p in (1, 2, 3):
         accumulate(mine[p])
     near(KEYS)
-    own_sends(OUTPUT, wo_ref)
     for p in (0, 1, 2, 3):
         from_sib(QUERY, p)
         accumulate(theirs[p])
     middle(QUERY)
+    all_dealt()
+    own_sends(OUTPUT, wo.at[s])
     middle(KEYS)
     for p in (4, 5, 6):
         accumulate(mine[p])
@@ -241,41 +297,6 @@
 
     query_at = lax.broadcasted_iota(jnp.int32, (ROWS, BLOCK), 0) + core * ROWS
     allowed = lax.broadcasted_iota(jnp.int32, (ROWS, BLOCK), 1) <= query_at
-    for h in range(HEADS_HERE):
-        scores = jnp.where(allowed, scores_of(h, chip), -1e30)
-        high = jnp.max(scores, axis=1, keepdims=True)
-        weights = jnp.exp2((scores - high) * SCORE_LOG2).astype(bf16)
-        oacc[h] = jnp.dot(weights, values_of(chip), preferred_element_type=f32)
-        macc[h] = jnp.broadcast_to(high, (ROWS, HEAD))
-
-    def attend(block, _):
-        values = values_of(block)
-        for h in range(HEADS_HERE):
-            scores = scores_of(h, block)
-            before = macc[h][:, :1]
-            high = jnp.maximum(before, jnp.max(scores, axis=1, keepdims=True))
-            weights = jnp.exp2((scores - high) * SCORE_LOG2).astype(bf16)
-            keep = jnp.exp2((before - high) * SCORE_LOG2)
-            oacc[h] = oacc[h] * keep + jnp.dot(weights, values, preferred_element_type=f32)
-            macc[h] = jnp.broadcast_to(high, (ROWS, HEAD))
-        return 0
-
-    near(OUTPUT)
-    lax.fori_loop(0, jnp.minimum(chip, 4), attend, 0)
-    middle(OUTPUT)
-    lax.fori_loop(4, jnp.maximum(chip, 4), attend, 0)
-    for h in range(HEADS_HERE):
-        attn[:, h * HEAD : (h + 1) * HEAD] = (oacc[h][:, :HEAD] / oacc[h][:, HEAD:]).astype(bf16)
-    far(OUTPUT)
-    load_o.wait()
-    for p in range(8):
-        from_sib(OUTPUT, p)
-
-    def partial(yi, zi):
-        return jnp.dot(attn[...], wo[wid(yi, zi)], preferred_element_type=f32)
-
-    order = (1 - yh, yh)
-
     def hop(label, source, place, peer):
         copy = pltpu.make_async_remote_copy(
             src_ref=source, dst_ref=place, send_sem=rsend.at[label], recv_sem=rrecv.at[label],
@@ -290,45 +311,88 @@
             device_id=to_sib, device_id_type=MESH,
         ).wait_recv()
 
-    halves = (pl.ds(0, 128), pl.ds(128, 128))
-    ways = (to_zp, to_zm)
-    for j in range(2):
-        snd4[j] = partial(order[j], lax.rem(z + 4, 8)).astype(bf16)
-        for way in range(2):
-            hop(way * 2 + j, snd4.at[j, halves[way]], rcv4.at[j, halves[way]], ways[way])
-    for d in (3, 2, 1):
-        for j in range(2):
-            for way in range(2):
-                at = lax.rem(z + d, 8) if way == 0 else lax.rem(z + 8 - d, 8)
-                term = partial(order[j], at)
-                if d == 3:
-                    landed(way * 2 + j, rcv4.at[j, halves[way]])
-                    got = rcv4[j, halves[way]].astype(f32)
-                    if way == 0:
-                        snd[d - 1, way, j, :128] = (term[:128] + got).astype(bf16)
-                        snd[d - 1, way, j, 128:] = term[128:].astype(bf16)
-                    else:
-                        snd[d - 1, way, j, :128] = term[:128].astype(bf16)
-                        snd[d - 1, way, j, 128:] = (term[128:] + got).astype(bf16)
-                else:
-                    landed((4 - d - 1) * 4 + way * 2 + j, rcv.at[d, way, j])
-                    snd[d - 1, way, j] = (term + rcv[d, way, j].astype(f32)).astype(bf16)
-                hop((4 - d) * 4 + way * 2 + j, snd.at[d - 1, way, j], rcv.at[d - 1, way, j], ways[way])
-    for j in range(2):
-        term = partial(order[j], z)
-        for way in range(2):
-            landed(12 + way * 2 + j, rcv.at[0, way, j])
-            term = term + rcv[0, way, j].astype(f32)
-        if j == 0:
-            ysnd[...] = term.astype(bf16)
-            hop(16, ysnd, yrcv, to_yh)
-        else:
-            columns = pl.ds(pl.multiple_of(w * BLOCK, BLOCK), BLOCK)
-            total[...] = term + hid[:, columns].astype(f32)
-    landed(16, yrcv)
-    out_ref[...] = (total[...] + yrcv[...].astype(f32)).astype(bf16)
+    def zplace(source, h, half=None):
+        return heads.at[source, h] if half is None else heads.at[source, h, pl.ds(half * 128, 128)]
+
+    def zsource(way, d):
+        return lax.rem(z + 8 - d, 8) if way == 0 else lax.rem(z + d, 8)
+
+    def zsend(h, way, d):
+        place = zplace(zsource(way, d - 1), h, way if d == 4 else None)
+        hop((h * 2 + way) * 4 + d - 1, place, place, (to_zp, to_zm)[way])
+
+    def zland(h, way, d):
+        landed((h * 2 + way) * 4 + d - 1, zplace(zsource(way, d), h, way if d == 4 else None))
+
+    def wave(turn):
+        for d in (1, 2, 3, 4):
+            h = turn - d
+            if 0 <= h < HEADS_HERE:
+                for way in range(2):
+                    zland(h, way, d)
+                    if d < 4:
+                        zsend(h, way, d + 1)
+
+    for h in range(HEADS_HERE):
+        scores = jnp.where(allowed, scores_of(h, chip), -1e30)
+        high = jnp.max(scores, axis=1, keepdims=True)
+        weights = jnp.exp2((scores - high) * SCORE_LOG2).astype(bf16)
+        oacc[...] = jnp.dot(weights, values_of(chip), preferred_element_type=f32)
+        macc[...] = jnp.broadcast_to(high, (ROWS, HEAD))
+
+        def attend(block, _, h=h):
+            scores = scores_of(h, block)
+            before = macc[:, :1]
+            high = jnp.maximum(before, jnp.max(scores, axis=1, keepdims=True))
+            weights = jnp.exp2((scores - high) * SCORE_LOG2).astype(bf16)
+            keep = jnp.exp2((before - high) * SCORE_LOG2)
+            oacc[...] = oacc[...] * keep + jnp.dot(weights, values_of(block), preferred_element_type=f32)
+            macc[...] = jnp.broadcast_to(high, (ROWS, HEAD))
+            return 0
+
+        lax.fori_loop(0, chip, attend, 0)
+        heads[z, h] = (oacc[:, :HEAD] / oacc[:, HEAD:]).astype(bf16)
+        zsend(h, 0, 1)
+        zsend(h, 1, 1)
+        wave(h)
+        if h == 1:
+            near(OUTPUT)
+        if h == 3:
+            middle(OUTPUT)
+    for turn in range(HEADS_HERE, HEADS_HERE + 4):
+        wave(turn)
+    far(OUTPUT)
+
+    def columns_from(p, fresh):
+        row, column = chips[p]
+        place = row * 2 + column
+        left = jnp.concatenate([heads[i, row] for i in range(8)], axis=1)
+        for yi in range(2):
+            right = jnp.concatenate(
+                [wo[place * 2 + i, yi].reshape(8 * HEAD, HEAD) for i in range(2)], axis=1
+            )
+            term = jnp.dot(left, right, preferred_element_type=f32)
+            tacc[yi, column] = term if fresh else tacc[yi, column] + term
+
+    for n, (column, positions) in enumerate(((yl, (0, 2, 3, 6)), (yp, (1, 4, 5, 7)))):
+        for p in positions:
+            from_sib(OUTPUT, p)
+            columns_from(p, p < 2)
+        ysnd[column] = tacc[1 - yh, column].astype(bf16)
+        hop(32 + n, ysnd.at[column], yrcv.at[column], to_yh)
+    for n, column in enumerate((yl, yp)):
+        landed(32 + n, yrcv.at[column])
+        at = pl.ds(pl.multiple_of(column * 256, 256), 256)
+        wide = pl.ds(pl.multiple_of(w * BLOCK + column * 256, 256), 256)
+        out_ref[:, at] = (hid[:, wide].astype(f32) + tacc[yh, column] + yrcv[column].astype(f32)).astype(bf16)
     for copy in started:
         copy.wait_send()
+    for i in range(1, SHARDS):
+        deal(i).wait_send()
+
+    @pl.when(jnp.logical_not(keeps_piece))
+    def _():
+        deal(0).wait_send()
 
 
 def local(hidden_states, norm_gain, query_weight, key_value_matrix, output_weight):
@@ -346,24 +410,22 @@
             pltpu.VMEM((SHARDS, ROWS, BLOCK), bf16),
             pltpu.VMEM((SHARDS, BLOCK, HEAD), bf16),
             pltpu.VMEM((SHARDS, BLOCK, BLOCK), bf16),
-            pltpu.VMEM((SHARDS, BLOCK, BLOCK), bf16),
+            pltpu.VMEM((SHARDS, 2, 8, HEAD, HEAD), bf16),
             pltpu.VMEM((2, SHARDS * ROWS, HEAD), bf16),
             pltpu.VMEM((ROWS, BLOCK), f32),
             pltpu.VMEM((HEADS_HERE, ROWS, HEAD), bf16),
-            pltpu.VMEM((HEADS_HERE, ROWS, HEAD), f32),
-            pltpu.VMEM((HEADS_HERE, ROWS, 2 * HEAD), f32),
-            pltpu.VMEM((ROWS, BLOCK), bf16),
-            pltpu.VMEM((2, ROWS, BLOCK), bf16),
-            pltpu.VMEM((2, ROWS, BLOCK), bf16),
-            pltpu.VMEM((3, 2, 2, ROWS, BLOCK), bf16),
-            pltpu.VMEM((3, 2, 2, ROWS, BLOCK), bf16),
-            pltpu.VMEM((ROWS, BLOCK), bf16),
-            pltpu.VMEM((ROWS, BLOCK), bf16),
-            pltpu.VMEM((ROWS, BLOCK), f32),
+            pltpu.VMEM((ROWS, HEAD), f32),
+            pltpu.VMEM((ROWS, 2 * HEAD), f32),
+            pltpu.VMEM((8, HEADS_HERE, ROWS, HEAD), bf16),
+            pltpu.VMEM((2, 2, ROWS, 256), f32),
+            pltpu.VMEM((2, ROWS, 256), bf16),
+            pltpu.VMEM((2, ROWS, 256), bf16),
             dma((4, 16)),
             dma((4, 16)),
-            dma((17,)),
-            dma((17,)),
+            dma((34,)),
+            dma((34,)),
+            dma((16,)),
+            dma((16,)),
             dma((1,)),
             dma((1,)),
             dma((4,)),

time: 164 us -> 168 us (1.024); the launches traced: 164 us -> 165 us
  no operation moved by 1% of the time
where the time goes in v2:
time: 168 us; the launch traced here: 165 us
  Pallas kernels  162 us (96%)
  local copies, waits for them, and re-layouts  3.02 us (2%)
    pallas_call x1, Pallas kernels, local(): pl.pallas_call(body, out_shape=jax.ShapeDtypeStruct((ROWS, BLOCK), bf16),...  162 us

profile of v2, /device:TPU:1, one launch (start us, length us, event | category | flops | bytes accessed | tf_op | source)
XLA Modules:
  0.0 165.3 jit_solution(209820927597952586)
XLA Ops:
  0.0 1.3 reshape.3.gain_ref
  1.4 162.3 %shard_map.91 = bf16[256,512]{1,0:T(8,128)(2,1)} custom-call(bf16[256,8192]{1,0:T(8,128)(2,1)} %hidden_ref.1, bf16[1,8192]{1,0:T(2,128)(2,1)} %reshape.3.gain_ref, bf16[512,512]{1,0:T(8,128)(2,1)} %wq_ref.1, bf16[512,2048]{1,0:T(8,128)(2,1)} %wkv_ref.1, bf16[512,512]{1,0:T(8,128)(2,1)} %wo_ref.1, f32[256,128]{1,0:T(8,128)} %constant.8.clone.cr_ref, ...), custom_call_target="tpu_custom_call" | custom-call | tf_op jit(solution)/shard_map/pallas_call | solution.py:403
  163.7 1.7 %copy.11 = bf16[256,512]{1,0:T(8,128)(2,1)} copy(bf16[256,512]{1,0:T(8,128)(2,1)} %shard_map.91) | data formatting | bytes 524288

commit v3 on v2

--- a/solution.py
+++ b/solution.py
@@ -26,13 +26,13 @@
     sign = np.concatenate([-np.ones(HEAD // 2), np.ones(HEAD // 2)])
     inner = np.arange(ROWS)[:, None] * wide[None, :]
     outer = (np.arange(SHARDS) * ROWS)[:, None] * wide[None, :]
-    tables = (np.cos(inner), np.sin(inner) * sign, np.cos(outer), np.sin(outer) * sign)
-    return [t.astype(np.float32) for t in tables]
+    outer = outer[:, None, :]
+    return [np.stack([np.cos(t), np.sin(t) * sign]).astype(np.float32) for t in (inner, outer)]
 
 
 def body(
-    hidden_ref, gain_ref, wq_ref, wkv_ref, wo_ref, cr_ref, sr_ref, cb_ref, sb_ref,
-    out_ref,
+    hidden_ref, gain_ref, wq_ref, wkv_ref, wo_ref, inner_ref, outer_ref, out_ref,
+    inner, outer,
     hid, normed, wkv, wq, wo, kv, qacc, qrot, macc, oacc, heads, tacc, ysnd, yrcv,
     gsend, grecv, rsend, rrecv, dsend, drecv, xsend, xrecv, lsem,
 ):
@@ -79,9 +79,13 @@
     )
     load_hidden = pltpu.make_async_copy(hidden_ref, hid, lsem.at[1])
     load_q = pltpu.make_async_copy(wq_ref, wq.at[s], lsem.at[2])
+    load_inner = pltpu.make_async_copy(inner_ref, inner, lsem.at[4])
+    load_outer = pltpu.make_async_copy(outer_ref.at[:, s], outer, lsem.at[5])
     first.start()
     load_hidden.start()
     load_q.start()
+    load_inner.start()
+    load_outer.start()
     pl.semaphore_wait(barrier, 7 + SHARDS - jnp.where(keeps_piece, 1, 0))
 
     stores = {KV_WEIGHT: wkv, QUERY: wq, OUTPUT: wo}
@@ -125,26 +129,30 @@
         for label, peer in ((0, to_xp), (1, to_xm), (2, to_y), (3, to_sib)):
             send(k, label, source, slot(k, s), peer)
 
-    def near(k):
+    def near_x(k):
         arrive(k, 0, mine[2])
         forward(k, 6, mine[2], to_xp, 0)
         arrive(k, 1, mine[3])
         forward(k, 7, mine[3], to_xm, 1)
+        for p in (2, 3):
+            forward(k, sib_label[p], mine[p], to_sib)
+
+    def near_y(k):
         arrive(k, 2, mine[1])
         forward(k, 4, mine[1], to_xp)
         forward(k, 5, mine[1], to_xm)
-        for p in (1, 2, 3):
-            forward(k, sib_label[p], mine[p], to_sib)
-
-    def middle(k):
+        forward(k, sib_label[1], mine[1], to_sib)
+
+    def opposite(k):
         arrive(k, 6, mine[6], 0)
         arrive(k, 7, mine[6], 1)
         forward(k, 8, mine[6], to_y)
         forward(k, sib_label[6], mine[6], to_sib)
-        arrive(k, 4, mine[4])
-        forward(k, sib_label[4], mine[4], to_sib)
-        arrive(k, 5, mine[5])
-        forward(k, sib_label[5], mine[5], to_sib)
+
+    def corners(k):
+        for label, p in ((4, 4), (5, 5)):
+            arrive(k, label, mine[p])
+            forward(k, sib_label[p], mine[p], to_sib)
 
     def far(k):
         arrive(k, 8, mine[7])
@@ -155,7 +163,6 @@
 
     first.wait()
     own_sends(KV_WEIGHT, wkv.at[s])
-    own_sends(QUERY, wq_ref)
 
     def piece(p):
         return wo_ref.at[
@@ -170,17 +177,6 @@
         )
 
     kept = pltpu.make_async_copy(piece(s), wo.at[s, lax.div(s, 8), z], lsem.at[3])
-    for i in range(1, SHARDS):
-        deal(i).start()
-
-    @pl.when(keeps_piece)
-    def _():
-        kept.start()
-
-    @pl.when(jnp.logical_not(keeps_piece))
-    def _():
-        deal(0).start()
-
     def dealt(label):
         place = wo.at[s, lax.div(label, 8), lax.rem(label, 8)]
         pltpu.make_async_remote_copy(
@@ -210,16 +206,30 @@
     squares = lax.fori_loop(0, SHARDS, square, jnp.zeros((ROWS, 128), f32))
     inverse = lax.rsqrt(jnp.sum(squares, axis=1, keepdims=True) * (1.0 / 8192.0) + 1e-05)
 
-    near(KV_WEIGHT)
+    near_x(KV_WEIGHT)
+    near_y(KV_WEIGHT)
+    own_sends(QUERY, wq_ref)
+    for i in range(1, SHARDS):
+        deal(i).start()
+
+    @pl.when(keeps_piece)
+    def _():
+        kept.start()
+
+    @pl.when(jnp.logical_not(keeps_piece))
+    def _():
+        deal(0).start()
+
 
     def scale(i, _):
         columns = pl.ds(pl.multiple_of(i * BLOCK, BLOCK), BLOCK)
-        block = hid[:, columns].astype(f32) * inverse * gain_ref[:, columns].astype(f32)
+        block = hid[:, columns].astype(f32) * inverse * gain_ref[columns].astype(f32)
         normed[i] = block.astype(bf16)
         return 0
 
     lax.fori_loop(0, SHARDS, scale, 0)
-    middle(KV_WEIGHT)
+    opposite(KV_WEIGHT)
+    corners(KV_WEIGHT)
     far(KV_WEIGHT)
 
     for p in range(8):
@@ -229,10 +239,10 @@
         return acc + jnp.dot(normed[i], wkv[i], preferred_element_type=f32)
 
     raw = lax.fori_loop(0, SHARDS, project, jnp.zeros((ROWS, HEAD), f32))
-    near(QUERY)
-    base = pl.ds(s, 1)
-    cosines = cb_ref[base, :] * cr_ref[...] - sb_ref[base, :] * sr_ref[...]
-    sines = sb_ref[base, :] * cr_ref[...] + cb_ref[base, :] * sr_ref[...]
+    load_inner.wait()
+    load_outer.wait()
+    cosines = outer[0] * inner[0] - outer[1] * inner[1]
+    sines = outer[1] * inner[0] + outer[0] * inner[1]
 
     def rotate(u):
         return u * cosines + pltpu.roll(u, HEAD // 2, 1) * sines
@@ -258,26 +268,34 @@
         recv_sem=xrecv.at[0], device_id=to_pair, device_id_type=MESH,
     ).wait_recv()
     own_sends(KEYS, slot(KEYS, s))
+    near_x(QUERY)
+    from_sib(QUERY, 0)
+    accumulate(theirs[0])
+    near_x(KEYS)
+    near_y(KEYS)
+    near_y(QUERY)
+    all_dealt()
+    own_sends(OUTPUT, wo.at[s])
     for p in (1, 2, 3):
         accumulate(mine[p])
-    near(KEYS)
-    for p in (0, 1, 2, 3):
+    opposite(KEYS)
+    corners(KEYS)
+    opposite(QUERY)
+    for p in (1, 2, 3):
         from_sib(QUERY, p)
         accumulate(theirs[p])
-    middle(QUERY)
-    all_dealt()
-    own_sends(OUTPUT, wo.at[s])
-    middle(KEYS)
-    for p in (4, 5, 6):
+    far(KEYS)
+    accumulate(mine[6])
+    from_sib(QUERY, 6)
+    accumulate(theirs[6])
+    corners(QUERY)
+    for p in (4, 5):
         accumulate(mine[p])
-    far(KEYS)
     far(QUERY)
-    for p in (4, 5, 6):
+    accumulate(mine[7])
+    for p in (4, 5, 7):
         from_sib(QUERY, p)
         accumulate(theirs[p])
-    accumulate(mine[7])
-    from_sib(QUERY, 7)
-    accumulate(theirs[7])
     for h in range(HEADS_HERE):
         qrot[h] = rotate(qacc[:, h * HEAD : (h + 1) * HEAD]).astype(bf16)
     for p in range(8):
@@ -333,34 +351,42 @@
                     if d < 4:
                         zsend(h, way, d + 1)
 
-    for h in range(HEADS_HERE):
-        scores = jnp.where(allowed, scores_of(h, chip), -1e30)
-        high = jnp.max(scores, axis=1, keepdims=True)
-        weights = jnp.exp2((scores - high) * SCORE_LOG2).astype(bf16)
-        oacc[...] = jnp.dot(weights, values_of(chip), preferred_element_type=f32)
-        macc[...] = jnp.broadcast_to(high, (ROWS, HEAD))
-
-        def attend(block, _, h=h):
-            scores = scores_of(h, block)
-            before = macc[:, :1]
-            high = jnp.maximum(before, jnp.max(scores, axis=1, keepdims=True))
+    for pair_first in (0, 2):
+        both = (pair_first, pair_first + 1)
+        for h in both:
+            scores = jnp.where(allowed, scores_of(h, chip), -1e30)
+            high = jnp.max(scores, axis=1, keepdims=True)
             weights = jnp.exp2((scores - high) * SCORE_LOG2).astype(bf16)
-            keep = jnp.exp2((before - high) * SCORE_LOG2)
-            oacc[...] = oacc[...] * keep + jnp.dot(weights, values_of(block), preferred_element_type=f32)
-            macc[...] = jnp.broadcast_to(high, (ROWS, HEAD))
+            oacc[h] = jnp.dot(weights, values_of(chip), preferred_element_type=f32)
+            macc[h] = jnp.broadcast_to(high, (ROWS, HEAD))
+
+        def attend(block, _, both=both):
+            values = values_of(block)
+            for h in both:
+                scores = scores_of(h, block)
+                before = macc[h][:, :1]
+                high = jnp.maximum(before, jnp.max(scores, axis=1, keepdims=True))
+                weights = jnp.exp2((scores - high) * SCORE_LOG2).astype(bf16)
+                keep = jnp.exp2((before - high) * SCORE_LOG2)
+                oacc[h] = oacc[h] * keep + jnp.dot(weights, values, preferred_element_type=f32)
+                macc[h] = jnp.broadcast_to(high, (ROWS, HEAD))
             return 0
 
         lax.fori_loop(0, chip, attend, 0)
-        heads[z, h] = (oacc[:, :HEAD] / oacc[:, HEAD:]).astype(bf16)
-        zsend(h, 0, 1)
-        zsend(h, 1, 1)
-        wave(h)
-        if h == 1:
-            near(OUTPUT)
-        if h == 3:
-            middle(OUTPUT)
+        for h in both:
+            heads[z, h] = (oacc[h][:, :HEAD] / oacc[h][:, HEAD:]).astype(bf16)
+            zsend(h, 0, 1)
+            zsend(h, 1, 1)
+        if pair_first == 0:
+            near_x(OUTPUT)
+            near_y(OUTPUT)
+            wave(1)
+    wave(2)
+    wave(3)
+    opposite(OUTPUT)
     for turn in range(HEADS_HERE, HEADS_HERE + 4):
         wave(turn)
+    corners(OUTPUT)
     far(OUTPUT)
 
     def columns_from(p, fresh):
@@ -403,9 +429,11 @@
     return pl.pallas_call(
         body,
         out_shape=jax.ShapeDtypeStruct((ROWS, BLOCK), bf16),
-        in_specs=[anywhere, inside, anywhere, anywhere, anywhere] + [inside] * 4,
+        in_specs=[anywhere, inside, anywhere, anywhere, anywhere] + [anywhere] * 2,
         out_specs=inside,
         scratch_shapes=[
+            pltpu.VMEM((2, ROWS, HEAD), f32),
+            pltpu.VMEM((2, 1, HEAD), f32),
             pltpu.VMEM((ROWS, 8192), bf16),
             pltpu.VMEM((SHARDS, ROWS, BLOCK), bf16),
             pltpu.VMEM((SHARDS, BLOCK, HEAD), bf16),
@@ -414,8 +442,8 @@
             pltpu.VMEM((2, SHARDS * ROWS, HEAD), bf16),
             pltpu.VMEM((ROWS, BLOCK), f32),
             pltpu.VMEM((HEADS_HERE, ROWS, HEAD), bf16),
-            pltpu.VMEM((ROWS, HEAD), f32),
-            pltpu.VMEM((ROWS, 2 * HEAD), f32),
+            pltpu.VMEM((HEADS_HERE, ROWS, HEAD), f32),
+            pltpu.VMEM((HEADS_HERE, ROWS, 2 * HEAD), f32),
             pltpu.VMEM((8, HEADS_HERE, ROWS, HEAD), bf16),
             pltpu.VMEM((2, 2, ROWS, 256), f32),
             pltpu.VMEM((2, ROWS, 256), bf16),
@@ -428,12 +456,12 @@
             dma((16,)),
             dma((1,)),
             dma((1,)),
-            dma((4,)),
+            dma((6,)),
         ],
         compiler_params=pltpu.CompilerParams(
             collective_id=0, has_side_effects=True, vmem_limit_bytes=56 * 1024 * 1024
         ),
-    )(hidden_states, norm_gain.reshape(1, -1), query_weight, key_value_matrix, output_weight, *tables)
+    )(hidden_states, norm_gain, query_weight, key_value_matrix, output_weight, *tables)
 
 
 def solution(mesh):

time: 168 us -> 138 us (0.82)
  the two profiles are of different devices: /device:TPU:1 before, /device:TPU:6 now
where the time goes in v3:
time: 138 us
  Pallas kernels  137 us (99%)
  local copies, waits for them, and re-layouts  1.67 us (1%)
    pallas_call x1, Pallas kernels, local(): pl.pallas_call(body, out_shape=jax.ShapeDtypeStruct((ROWS, BLOCK), bf16),...  137 us

profile of v3, /device:TPU:6, one launch (start us, length us, event | category | flops | bytes accessed | tf_op | source)
XLA Modules:
  0.0 138.2 jit_solution(4015188263836702993)
XLA Ops:
  0.0 136.5 %shard_map.73 = bf16[256,512]{1,0:T(8,128)(2,1)} custom-call(bf16[256,8192]{1,0:T(8,128)(2,1)} %hidden_ref.1, bf16[8192]{0:T(1024)(128)(2,1)} %gain_ref.1, bf16[512,512]{1,0:T(8,128)(2,1)} %wq_ref.1, bf16[512,2048]{1,0:T(8,128)(2,1)} %wkv_ref.1, bf16[512,512]{1,0:T(8,128)(2,1)} %wo_ref.1, f32[2,256,128]{2,1,0:T(8,128)} %constant.4.clone.inner_ref, ...), custom_call_target="tpu_custom_call" | custom-call | tf_op jit(solution)/shard_map/pallas_call | solution.py:429
  136.5 1.7 %copy.9 = bf16[256,512]{1,0:T(8,128)(2,1)} copy(bf16[256,512]{1,0:T(8,128)(2,1)} %shard_map.73) | data formatting | bytes 524288

commit v4 on v3

--- a/solution.py
+++ b/solution.py
@@ -33,7 +33,7 @@
 def body(
     hidden_ref, gain_ref, wq_ref, wkv_ref, wo_ref, inner_ref, outer_ref, out_ref,
     inner, outer,
-    hid, normed, wkv, wq, wo, kv, qacc, qrot, macc, oacc, heads, tacc, ysnd, yrcv,
+    hid, normed, wkv, wq, wo, pieces, kv, qacc, qrot, macc, oacc, heads, tacc, ysnd, yrcv,
     gsend, grecv, rsend, rrecv, dsend, drecv, xsend, xrecv, lsem,
 ):
     s = lax.axis_index("seq")
@@ -60,19 +60,12 @@
     barrier = pltpu.get_barrier_semaphore()
     for peer in (to_xp, to_xm, to_y, to_sib, to_zp, to_zm, to_yh):
         pl.semaphore_signal(barrier, inc=1, device_id=peer, device_id_type=MESH)
-    keeps_piece = lax.rem(s, 8) == z
-    deal_label = lax.div(s, 8) * 8 + z
-
-    def greet(label):
-        dealer = (z + 8 * lax.div(label, 8), wid(yh, lax.rem(label, 8)))
-        pl.semaphore_signal(barrier, inc=1, device_id=dealer, device_id_type=MESH)
-
-    for i in range(1, SHARDS):
-        greet(lax.rem(deal_label + i, SHARDS))
-
-    @pl.when(jnp.logical_not(keeps_piece))
-    def _():
-        greet(deal_label)
+    plane = [(sid(xi, yi, ci), w) for xi in (x, xp, xm, xo) for yi in (yl, yp) for ci in (core, sib_core)]
+    ring = [lax.rem(z + d, 8) for d in range(8)]
+    others = [peer for n, peer in enumerate(plane) if n not in (0, 1, 2, 4, 8)]
+    others += [(s, wid(yh, ring[d])) for d in range(2, 7)]
+    for peer in others:
+        pl.semaphore_signal(barrier, inc=1, device_id=peer, device_id_type=MESH)
 
     first = pltpu.make_async_copy(
         wkv_ref.at[:, pl.ds(pl.multiple_of(w * HEAD, HEAD), HEAD)], wkv.at[s], lsem.at[0]
@@ -86,7 +79,7 @@
     load_q.start()
     load_inner.start()
     load_outer.start()
-    pl.semaphore_wait(barrier, 7 + SHARDS - jnp.where(keeps_piece, 1, 0))
+    pl.semaphore_wait(barrier, 7 + len(others))
 
     stores = {KV_WEIGHT: wkv, QUERY: wq, OUTPUT: wo}
 
@@ -125,9 +118,16 @@
     theirs = [sid(a, b, sib_core) for a, b in chips]
     sib_label = [3, 9, 10, 11, 12, 13, 14, 15]
 
+    def own_x(k, source):
+        for label, peer in ((0, to_xp), (1, to_xm), (3, to_sib)):
+            send(k, label, source, slot(k, s), peer)
+
+    def own_y(k, source):
+        send(k, 2, source, slot(k, s), to_y)
+
     def own_sends(k, source):
-        for label, peer in ((0, to_xp), (1, to_xm), (2, to_y), (3, to_sib)):
-            send(k, label, source, slot(k, s), peer)
+        own_x(k, source)
+        own_y(k, source)
 
     def near_x(k):
         arrive(k, 0, mine[2])
@@ -169,32 +169,41 @@
             pl.ds(pl.multiple_of(lax.div(p, 4) * HEAD, HEAD), HEAD), pl.ds(pl.multiple_of(lax.rem(p, 4) * HEAD, HEAD), HEAD)
         ]
 
-    def deal(i):
-        p = lax.rem(s + i, SHARDS)
-        return pltpu.make_async_remote_copy(
-            src_ref=piece(p), dst_ref=wo.at[p, lax.div(s, 8), z], send_sem=dsend.at[i], recv_sem=drecv.at[deal_label],
-            device_id=(p, wid(yh, lax.rem(s, 8))), device_id_type=MESH,
+    def part(label, source, place, peer):
+        copy = pltpu.make_async_remote_copy(
+            src_ref=source, dst_ref=place, send_sem=dsend.at[label], recv_sem=drecv.at[label],
+            device_id=peer, device_id_type=MESH,
         )
-
-    kept = pltpu.make_async_copy(piece(s), wo.at[s, lax.div(s, 8), z], lsem.at[3])
-    def dealt(label):
-        place = wo.at[s, lax.div(label, 8), lax.rem(label, 8)]
-        pltpu.make_async_remote_copy(
-            src_ref=place, dst_ref=place, send_sem=dsend.at[0], recv_sem=drecv.at[label], device_id=to_sib,
-            device_id_type=MESH,
-        ).wait_recv()
+        return copy
+
+    keep_piece = pltpu.make_async_copy(piece(s), pieces.at[lax.div(s, 8), lax.rem(s, 8)], lsem.at[3])
+    keep_rows = pltpu.make_async_copy(pieces.at[:, z], wo.at[s, :, z], lsem.at[2])
+
+    def spread():
+        keep_piece.start()
+        for n in range(1, SHARDS):
+            copy = part(n, piece(plane[n][0]), pieces.at[lax.div(s, 8), lax.rem(s, 8)], plane[n])
+            copy.start()
+            started.append(copy)
+
+    senders = [(sid(xi, yi, ci), w) for xi in (x, xm, xp, xo) for yi in (yl, yp) for ci in (core, sib_core)]
+
+    def deal():
+        keep_piece.wait()
+        for n in range(1, SHARDS):
+            place = pieces.at[lax.div(senders[n][0], 8), lax.rem(senders[n][0], 8)]
+            part(n, place, place, to_sib).wait_recv()
+        keep_rows.start()
+        for d in (4, 3, 5, 2, 6, 1, 7):
+            copy = part(15 + d, pieces.at[:, ring[d]], wo.at[s, :, z], (s, wid(yh, ring[d])))
+            copy.start()
+            started.append(copy)
 
     def all_dealt():
-        for i in range(1, SHARDS):
-            dealt(lax.rem(deal_label + i, SHARDS))
-
-        @pl.when(keeps_piece)
-        def _():
-            kept.wait()
-
-        @pl.when(jnp.logical_not(keeps_piece))
-        def _():
-            dealt(deal_label)
+        keep_rows.wait()
+        for d in range(1, 8):
+            place = wo.at[s, :, ring[8 - d]]
+            part(15 + d, place, place, to_sib).wait_recv()
 
     load_hidden.wait()
 
@@ -208,17 +217,9 @@
 
     near_x(KV_WEIGHT)
     near_y(KV_WEIGHT)
-    own_sends(QUERY, wq_ref)
-    for i in range(1, SHARDS):
-        deal(i).start()
-
-    @pl.when(keeps_piece)
-    def _():
-        kept.start()
-
-    @pl.when(jnp.logical_not(keeps_piece))
-    def _():
-        deal(0).start()
+    own_x(QUERY, wq_ref)
+    opposite(KV_WEIGHT)
+    own_y(QUERY, wq_ref)
 
 
     def scale(i, _):
@@ -228,7 +229,6 @@
         return 0
 
     lax.fori_loop(0, SHARDS, scale, 0)
-    opposite(KV_WEIGHT)
     corners(KV_WEIGHT)
     far(KV_WEIGHT)
 
@@ -268,23 +268,26 @@
         recv_sem=xrecv.at[0], device_id=to_pair, device_id_type=MESH,
     ).wait_recv()
     own_sends(KEYS, slot(KEYS, s))
+    spread()
     near_x(QUERY)
     from_sib(QUERY, 0)
     accumulate(theirs[0])
     near_x(KEYS)
     near_y(KEYS)
     near_y(QUERY)
-    all_dealt()
-    own_sends(OUTPUT, wo.at[s])
-    for p in (1, 2, 3):
-        accumulate(mine[p])
-    opposite(KEYS)
-    corners(KEYS)
-    opposite(QUERY)
+    accumulate(mine[1])
+    accumulate(mine[2])
+    deal()
+    accumulate(mine[3])
     for p in (1, 2, 3):
         from_sib(QUERY, p)
         accumulate(theirs[p])
+    opposite(QUERY)
+    opposite(KEYS)
+    corners(KEYS)
     far(KEYS)
+    all_dealt()
+    own_sends(OUTPUT, wo.at[s])
     accumulate(mine[6])
     from_sib(QUERY, 6)
     accumulate(theirs[6])
@@ -342,14 +345,12 @@
     def zland(h, way, d):
         landed((h * 2 + way) * 4 + d - 1, zplace(zsource(way, d), h, way if d == 4 else None))
 
-    def wave(turn):
-        for d in (1, 2, 3, 4):
-            h = turn - d
-            if 0 <= h < HEADS_HERE:
-                for way in range(2):
-                    zland(h, way, d)
-                    if d < 4:
-                        zsend(h, way, d + 1)
+    def zstep(first, d):
+        for h in (first, first + 1):
+            for way in range(2):
+                zland(h, way, d)
+                if d < 4:
+                    zsend(h, way, d + 1)
 
     for pair_first in (0, 2):
         both = (pair_first, pair_first + 1)
@@ -372,20 +373,24 @@
                 macc[h] = jnp.broadcast_to(high, (ROWS, HEAD))
             return 0
 
-        lax.fori_loop(0, chip, attend, 0)
+        lax.fori_loop(0, jnp.minimum(chip, 4), attend, 0)
+        if pair_first == 2:
+            zstep(0, 1)
+            near_x(OUTPUT)
+            near_y(OUTPUT)
+        lax.fori_loop(4, jnp.maximum(chip, 4), attend, 0)
         for h in both:
             heads[z, h] = (oacc[h][:, :HEAD] / oacc[h][:, HEAD:]).astype(bf16)
             zsend(h, 0, 1)
             zsend(h, 1, 1)
-        if pair_first == 0:
-            near_x(OUTPUT)
-            near_y(OUTPUT)
-            wave(1)
-    wave(2)
-    wave(3)
+    zstep(0, 2)
+    zstep(2, 1)
     opposite(OUTPUT)
-    for turn in range(HEADS_HERE, HEADS_HERE + 4):
-        wave(turn)
+    zstep(0, 3)
+    zstep(2, 2)
+    zstep(0, 4)
+    zstep(2, 3)
+    zstep(2, 4)
     corners(OUTPUT)
     far(OUTPUT)
 
@@ -413,12 +418,6 @@
         out_ref[:, at] = (hid[:, wide].astype(f32) + tacc[yh, column] + yrcv[column].astype(f32)).astype(bf16)
     for copy in started:
         copy.wait_send()
-    for i in range(1, SHARDS):
-        deal(i).wait_send()
-
-    @pl.when(jnp.logical_not(keeps_piece))
-    def _():
-        deal(0).wait_send()
 
 
 def local(hidden_states, norm_gain, query_weight, key_value_matrix, output_weight):
@@ -439,6 +438,7 @@
             pltpu.VMEM((SHARDS, BLOCK, HEAD), bf16),
             pltpu.VMEM((SHARDS, BLOCK, BLOCK), bf16),
             pltpu.VMEM((SHARDS, 2, 8, HEAD, HEAD), bf16),
+            pltpu.VMEM((2, 8, HEAD, HEAD), bf16),
             pltpu.VMEM((2, SHARDS * ROWS, HEAD), bf16),
             pltpu.VMEM((ROWS, BLOCK), f32),
             pltpu.VMEM((HEADS_HERE, ROWS, HEAD), bf16),
@@ -452,8 +452,8 @@
             dma((4, 16)),
             dma((34,)),
             dma((34,)),
-            dma((16,)),
-            dma((16,)),
+            dma((23,)),
+            dma((23,)),
             dma((1,)),
             dma((1,)),
             dma((6,)),

time: 138 us -> 117 us (0.85)
  the two profiles are of different devices: /device:TPU:6 before, /device:TPU:1 now
where the time goes in v4:
time: 117 us; the launch traced here: 116 us
  Pallas kernels  115 us (98%)
  local copies, waits for them, and re-layouts  1.67 us (1%)
    pallas_call x1, Pallas kernels, local(): pl.pallas_call(body, out_shape=jax.ShapeDtypeStruct((ROWS, BLOCK), bf16),...  115 us

profile of v4, /device:TPU:1, one launch (start us, length us, event | category | flops | bytes accessed | tf_op | source)
XLA Modules:
  0.0 116.5 jit_solution(7029438204241659466)
XLA Ops:
  0.0 114.8 %shard_map.73 = bf16[256,512]{1,0:T(8,128)(2,1)} custom-call(bf16[256,8192]{1,0:T(8,128)(2,1)} %hidden_ref.1, bf16[8192]{0:T(1024)(128)(2,1)} %gain_ref.1, bf16[512,512]{1,0:T(8,128)(2,1)} %wq_ref.1, bf16[512,2048]{1,0:T(8,128)(2,1)} %wkv_ref.1, bf16[512,512]{1,0:T(8,128)(2,1)} %wo_ref.1, f32[2,256,128]{2,1,0:T(8,128)} %constant.4.clone.inner_ref, ...), custom_call_target="tpu_custom_call" | custom-call | tf_op jit(solution)/shard_map/pallas_call | solution.py:428
  114.8 1.7 %copy.9 = bf16[256,512]{1,0:T(8,128)(2,1)} copy(bf16[256,512]{1,0:T(8,128)(2,1)} %shard_map.73) | data formatting | bytes 524288

commit v5 on v4

--- a/solution.py
+++ b/solution.py
@@ -205,6 +205,8 @@
             place = wo.at[s, :, ring[8 - d]]
             part(15 + d, place, place, to_sib).wait_recv()
 
+    spread()
+
     load_hidden.wait()
 
     def square(i, acc):
@@ -268,7 +270,7 @@
         recv_sem=xrecv.at[0], device_id=to_pair, device_id_type=MESH,
     ).wait_recv()
     own_sends(KEYS, slot(KEYS, s))
-    spread()
+    deal()
     near_x(QUERY)
     from_sib(QUERY, 0)
     accumulate(theirs[0])
@@ -277,7 +279,6 @@
     near_y(QUERY)
     accumulate(mine[1])
     accumulate(mine[2])
-    deal()
     accumulate(mine[3])
     for p in (1, 2, 3):
         from_sib(QUERY, p)
@@ -352,6 +353,7 @@
                 if d < 4:
                     zsend(h, way, d + 1)
 
+    odd, doubles = lax.rem(chip, 2), lax.div(chip, 2)
     for pair_first in (0, 2):
         both = (pair_first, pair_first + 1)
         for h in both:
@@ -361,24 +363,39 @@
             oacc[h] = jnp.dot(weights, values_of(chip), preferred_element_type=f32)
             macc[h] = jnp.broadcast_to(high, (ROWS, HEAD))
 
-        def attend(block, _, both=both):
-            values = values_of(block)
+        def attend(first, width, both=both):
+            blocks = range(width)
+            values = [values_of(first + i) for i in blocks]
             for h in both:
-                scores = scores_of(h, block)
+                scores = [scores_of(h, first + i) for i in blocks]
                 before = macc[h][:, :1]
-                high = jnp.maximum(before, jnp.max(scores, axis=1, keepdims=True))
-                weights = jnp.exp2((scores - high) * SCORE_LOG2).astype(bf16)
+                peak = scores[0]
+                for more in scores[1:]:
+                    peak = jnp.maximum(peak, more)
+                high = jnp.maximum(before, jnp.max(peak, axis=1, keepdims=True))
                 keep = jnp.exp2((before - high) * SCORE_LOG2)
-                oacc[h] = oacc[h] * keep + jnp.dot(weights, values, preferred_element_type=f32)
+                mixed = oacc[h] * keep
+                for i in blocks:
+                    weights = jnp.exp2((scores[i] - high) * SCORE_LOG2).astype(bf16)
+                    mixed = mixed + jnp.dot(weights, values[i], preferred_element_type=f32)
+                oacc[h] = mixed
                 macc[h] = jnp.broadcast_to(high, (ROWS, HEAD))
+
+        def attend_one(block, _):
+            attend(block, 1)
             return 0
 
-        lax.fori_loop(0, jnp.minimum(chip, 4), attend, 0)
+        def attend_two(i, _):
+            attend(odd + 2 * i, 2)
+            return 0
+
+        lax.fori_loop(0, odd, attend_one, 0)
+        lax.fori_loop(0, jnp.minimum(doubles, 2), attend_two, 0)
         if pair_first == 2:
             zstep(0, 1)
             near_x(OUTPUT)
             near_y(OUTPUT)
-        lax.fori_loop(4, jnp.maximum(chip, 4), attend, 0)
+        lax.fori_loop(2, jnp.maximum(doubles, 2), attend_two, 0)
         for h in both:
             heads[z, h] = (oacc[h][:, :HEAD] / oacc[h][:, HEAD:]).astype(bf16)
             zsend(h, 0, 1)
@@ -391,8 +408,6 @@
     zstep(0, 4)
     zstep(2, 3)
     zstep(2, 4)
-    corners(OUTPUT)
-    far(OUTPUT)
 
     def columns_from(p, fresh):
         row, column = chips[p]
@@ -405,12 +420,26 @@
             term = jnp.dot(left, right, preferred_element_type=f32)
             tacc[yi, column] = term if fresh else tacc[yi, column] + term
 
-    for n, (column, positions) in enumerate(((yl, (0, 2, 3, 6)), (yp, (1, 4, 5, 7)))):
-        for p in positions:
-            from_sib(OUTPUT, p)
-            columns_from(p, p < 2)
+    def hand_over(n, column):
         ysnd[column] = tacc[1 - yh, column].astype(bf16)
         hop(32 + n, ysnd.at[column], yrcv.at[column], to_yh)
+
+    for p in (0, 2, 3):
+        from_sib(OUTPUT, p)
+        columns_from(p, p == 0)
+    from_sib(OUTPUT, 6)
+    columns_from(6, False)
+    hand_over(0, yl)
+    from_sib(OUTPUT, 1)
+    columns_from(1, True)
+    corners(OUTPUT)
+    for p in (4, 5):
+        from_sib(OUTPUT, p)
+        columns_from(p, False)
+    far(OUTPUT)
+    from_sib(OUTPUT, 7)
+    columns_from(7, False)
+    hand_over(1, yp)
     for n, column in enumerate((yl, yp)):
         landed(32 + n, yrcv.at[column])
         at = pl.ds(pl.multiple_of(column * 256, 256), 256)

time: 117 us -> 113 us (0.966)
  Pallas kernels: 115 us -> 111 us
    pallas_call x1, Pallas kernels: 115 us -> 111 us  [local(): pl.pallas_call(body, out_shape=jax.ShapeDtypeStruct((ROWS, BLOCK), bf16),...]
where the time goes in v5:
time: 113 us
  Pallas kernels  111 us (98%)
  local copies, waits for them, and re-layouts  1.67 us (1%)
    pallas_call x1, Pallas kernels, local(): pl.pallas_call(body, out_shape=jax.ShapeDtypeStruct((ROWS, BLOCK), bf16),...  111 us

profile of v5, /device:TPU:1, one launch (start us, length us, event | category | flops | bytes accessed | tf_op | source)
XLA Modules:
  0.0 113.0 jit_solution(1676515202582334525)
XLA Ops:
  0.0 111.3 %shard_map.73 = bf16[256,512]{1,0:T(8,128)(2,1)} custom-call(bf16[256,8192]{1,0:T(8,128)(2,1)} %hidden_ref.1, bf16[8192]{0:T(1024)(128)(2,1)} %gain_ref.1, bf16[512,512]{1,0:T(8,128)(2,1)} %wq_ref.1, bf16[512,2048]{1,0:T(8,128)(2,1)} %wkv_ref.1, bf16[512,512]{1,0:T(8,128)(2,1)} %wo_ref.1, f32[2,256,128]{2,1,0:T(8,128)} %constant.4.clone.inner_ref, ...), custom_call_target="tpu_custom_call" | custom-call | tf_op jit(solution)/shard_map/pallas_call | solution.py:457
  111.3 1.7 %copy.9 = bf16[256,512]{1,0:T(8,128)(2,1)} copy(bf16[256,512]{1,0:T(8,128)(2,1)} %shard_map.73) | data formatting | bytes 524288

commit v6 on v5

--- a/solution.py
+++ b/solution.py
@@ -16,6 +16,7 @@
 HEADS_HERE = 4
 SCORE_LOG2 = math.log2(math.e) / math.sqrt(HEAD)
 KV_WEIGHT, QUERY, OUTPUT, KEYS = 0, 1, 2, 3
+MAIN, PART = 2, 3
 f32 = jnp.float32
 bf16 = jnp.bfloat16
 
@@ -89,6 +90,10 @@
             return kv.at[:, rows] if half is None else kv.at[half, rows]
         if half is None:
             return stores[k].at[shard]
+        if half in (MAIN, PART):
+            if k == OUTPUT:
+                return wo.at[shard, :, pl.ds(0, 7) if half == MAIN else pl.ds(7, 1)]
+            return stores[k].at[shard, pl.ds(0, 448) if half == MAIN else pl.ds(448, 64)]
         if k == OUTPUT:
             return wo.at[shard, half]
         return stores[k].at[shard, pl.ds(half * 256, 256)]
@@ -130,17 +135,19 @@
         own_y(k, source)
 
     def near_x(k):
-        arrive(k, 0, mine[2])
-        forward(k, 6, mine[2], to_xp, 0)
-        arrive(k, 1, mine[3])
-        forward(k, 7, mine[3], to_xm, 1)
+        for label, p, peer in ((0, 2, to_xp), (1, 3, to_xm)):
+            arrive(k, label, mine[p])
+            forward(k, 6 + label, mine[p], peer, label)
+            if k in (QUERY, OUTPUT):
+                forward(k, 16 + label, mine[p], to_y, PART)
         for p in (2, 3):
             forward(k, sib_label[p], mine[p], to_sib)
 
     def near_y(k):
         arrive(k, 2, mine[1])
-        forward(k, 4, mine[1], to_xp)
-        forward(k, 5, mine[1], to_xm)
+        main = MAIN if k in (QUERY, OUTPUT) else None
+        forward(k, 4, mine[1], to_xp, main)
+        forward(k, 5, mine[1], to_xm, main)
         forward(k, sib_label[1], mine[1], to_sib)
 
     def opposite(k):
@@ -151,7 +158,11 @@
 
     def corners(k):
         for label, p in ((4, 4), (5, 5)):
-            arrive(k, label, mine[p])
+            if k in (QUERY, OUTPUT):
+                arrive(k, label, mine[p], MAIN)
+                arrive(k, label + 12, mine[p], PART)
+            else:
+                arrive(k, label, mine[p])
             forward(k, sib_label[p], mine[p], to_sib)
 
     def far(k):
@@ -283,12 +294,12 @@
     for p in (1, 2, 3):
         from_sib(QUERY, p)
         accumulate(theirs[p])
+    opposite(KEYS)
     opposite(QUERY)
-    opposite(KEYS)
     corners(KEYS)
-    far(KEYS)
     all_dealt()
     own_sends(OUTPUT, wo.at[s])
+    far(KEYS)
     accumulate(mine[6])
     from_sib(QUERY, 6)
     accumulate(theirs[6])
@@ -307,10 +318,12 @@
 
     ones = jnp.ones((BLOCK, HEAD), bf16)
 
+    turns = (x, xm, xp, xo)
+
     def scores_of(h, block):
         rows = pl.ds(pl.multiple_of(block * BLOCK, BLOCK), BLOCK)
         return lax.dot_general(
-            qrot[h], kv[0, rows], (((1,), (1,)), ((), ())), preferred_element_type=f32
+            qrot[turns[h]], kv[0, rows], (((1,), (1,)), ((), ())), preferred_element_type=f32
         )
 
     def values_of(block):
@@ -334,7 +347,8 @@
         ).wait_recv()
 
     def zplace(source, h, half=None):
-        return heads.at[source, h] if half is None else heads.at[source, h, pl.ds(half * 128, 128)]
+        whole = heads.at[source, turns[h]]
+        return whole if half is None else heads.at[source, turns[h], pl.ds(half * 128, 128)]
 
     def zsource(way, d):
         return lax.rem(z + 8 - d, 8) if way == 0 else lax.rem(z + d, 8)
@@ -397,18 +411,9 @@
             near_y(OUTPUT)
         lax.fori_loop(2, jnp.maximum(doubles, 2), attend_two, 0)
         for h in both:
-            heads[z, h] = (oacc[h][:, :HEAD] / oacc[h][:, HEAD:]).astype(bf16)
+            heads[z, turns[h]] = (oacc[h][:, :HEAD] / oacc[h][:, HEAD:]).astype(bf16)
             zsend(h, 0, 1)
             zsend(h, 1, 1)
-    zstep(0, 2)
-    zstep(2, 1)
-    opposite(OUTPUT)
-    zstep(0, 3)
-    zstep(2, 2)
-    zstep(0, 4)
-    zstep(2, 3)
-    zstep(2, 4)
-
     def columns_from(p, fresh):
         row, column = chips[p]
         place = row * 2 + column
@@ -420,18 +425,26 @@
             term = jnp.dot(left, right, preferred_element_type=f32)
             tacc[yi, column] = term if fresh else tacc[yi, column] + term
 
+    zstep(0, 2)
+    zstep(2, 1)
+    opposite(OUTPUT)
+    zstep(0, 3)
+    zstep(2, 2)
+    zstep(0, 4)
+    zstep(2, 3)
+    for p, fresh in ((0, True), (2, False), (1, True)):
+        from_sib(OUTPUT, p)
+        columns_from(p, fresh)
+    zstep(2, 4)
+
     def hand_over(n, column):
         ysnd[column] = tacc[1 - yh, column].astype(bf16)
         hop(32 + n, ysnd.at[column], yrcv.at[column], to_yh)
 
-    for p in (0, 2, 3):
+    for p in (3, 6):
         from_sib(OUTPUT, p)
-        columns_from(p, p == 0)
-    from_sib(OUTPUT, 6)
-    columns_from(6, False)
+        columns_from(p, False)
     hand_over(0, yl)
-    from_sib(OUTPUT, 1)
-    columns_from(1, True)
     corners(OUTPUT)
     for p in (4, 5):
         from_sib(OUTPUT, p)
@@ -477,8 +490,8 @@
             pltpu.VMEM((2, 2, ROWS, 256), f32),
             pltpu.VMEM((2, ROWS, 256), bf16),
             pltpu.VMEM((2, ROWS, 256), bf16),
-            dma((4, 16)),
-            dma((4, 16)),
+            dma((4, 18)),
+            dma((4, 18)),
             dma((34,)),
             dma((34,)),
             dma((23,)),

time: 113 us -> 113 us (level)
  no operation moved by 1% of the time
where the time goes in v6:
time: 113 us; the launch traced here: 112 us
  Pallas kernels  111 us (98%)
  local copies, waits for them, and re-layouts  1.67 us (1%)
    pallas_call x1, Pallas kernels, local(): pl.pallas_call(body, out_shape=jax.ShapeDtypeStruct((ROWS, BLOCK), bf16),...  111 us

profile of v6, /device:TPU:1, one launch (start us, length us, event | category | flops | bytes accessed | tf_op | source)
XLA Modules:
  0.0 112.5 jit_solution(8834638546858869459)
XLA Ops:
  0.0 110.8 %shard_map.73 = bf16[256,512]{1,0:T(8,128)(2,1)} custom-call(bf16[256,8192]{1,0:T(8,128)(2,1)} %hidden_ref.1, bf16[8192]{0:T(1024)(128)(2,1)} %gain_ref.1, bf16[512,512]{1,0:T(8,128)(2,1)} %wq_ref.1, bf16[512,2048]{1,0:T(8,128)(2,1)} %wkv_ref.1, bf16[512,512]{1,0:T(8,128)(2,1)} %wo_ref.1, f32[2,256,128]{2,1,0:T(8,128)} %constant.4.clone.inner_ref, ...), custom_call_target="tpu_custom_call" | custom-call | tf_op jit(solution)/shard_map/pallas_call | solution.py:470
  110.8 1.7 %copy.9 = bf16[256,512]{1,0:T(8,128)(2,1)} copy(bf16[256,512]{1,0:T(8,128)(2,1)} %shard_map.73) | data formatting | bytes 524288

commit v7 on v6

--- a/solution.py
+++ b/solution.py
@@ -414,11 +414,11 @@
             heads[z, turns[h]] = (oacc[h][:, :HEAD] / oacc[h][:, HEAD:]).astype(bf16)
             zsend(h, 0, 1)
             zsend(h, 1, 1)
-    def columns_from(p, fresh):
+    def columns_from(p, fresh, sides=(0, 1)):
         row, column = chips[p]
         place = row * 2 + column
         left = jnp.concatenate([heads[i, row] for i in range(8)], axis=1)
-        for yi in range(2):
+        for yi in sides:
             right = jnp.concatenate(
                 [wo[place * 2 + i, yi].reshape(8 * HEAD, HEAD) for i in range(2)], axis=1
             )
@@ -451,8 +451,9 @@
         columns_from(p, False)
     far(OUTPUT)
     from_sib(OUTPUT, 7)
-    columns_from(7, False)
+    columns_from(7, False, (1 - yh,))
     hand_over(1, yp)
+    columns_from(7, False, (yh,))
     for n, column in enumerate((yl, yp)):
         landed(32 + n, yrcv.at[column])
         at = pl.ds(pl.multiple_of(column * 256, 256), 256)

time: 113 us -> 113 us (level)
  no operation moved by 1% of the time
where the time goes in v7:
time: 113 us; the launch traced here: 112 us
  Pallas kernels  111 us (98%)
  local copies, waits for them, and re-layouts  1.67 us (1%)
    pallas_call x1, Pallas kernels, local(): pl.pallas_call(body, out_shape=jax.ShapeDtypeStruct((ROWS, BLOCK), bf16),...  111 us

profile of v7, /device:TPU:1, one launch (start us, length us, event | category | flops | bytes accessed | tf_op | source)
XLA Modules:
  0.0 112.4 jit_solution(3722556819610668538)
XLA Ops:
  0.0 110.8 %shard_map.73 = bf16[256,512]{1,0:T(8,128)(2,1)} custom-call(bf16[256,8192]{1,0:T(8,128)(2,1)} %hidden_ref.1, bf16[8192]{0:T(1024)(128)(2,1)} %gain_ref.1, bf16[512,512]{1,0:T(8,128)(2,1)} %wq_ref.1, bf16[512,2048]{1,0:T(8,128)(2,1)} %wkv_ref.1, bf16[512,512]{1,0:T(8,128)(2,1)} %wo_ref.1, f32[2,256,128]{2,1,0:T(8,128)} %constant.4.clone.inner_ref, ...), custom_call_target="tpu_custom_call" | custom-call | tf_op jit(solution)/shard_map/pallas_call | solution.py:471
  110.8 1.7 %copy.9 = bf16[256,512]{1,0:T(8,128)(2,1)} copy(bf16[256,512]{1,0:T(8,128)(2,1)} %shard_map.73) | data formatting | bytes 524288
